TPU v7x, 512 devices: a whole 4x4x16 slice. The times are simulated.
512 devices in a mesh: pipe: 32 (over x, z_lo), dp: 2 (over z_hi), tensor: 8 (over y, core).
Axes of the slice: x: 4, y: 4, z: 16 (z_hi: 2, z_lo: 8; z = z_hi * 8 + z_lo), core: 2. Of those that a mesh axis runs over, the one named last changes fastest.
Arguments:
- acts_in: bfloat16 [32, 2, 2, 96, 2048], P('pipe', 'dp', None, 'tensor'), may hold values from -6 to 6
- saved_in: bfloat16 [32, 2, 2, 96, 2048], P('pipe', 'dp', None, 'tensor'), may hold values from -6 to 6
- out_grad: bfloat16 [32, 2, 2, 96, 2048], P('pipe', 'dp', None, 'tensor'), may hold values from -1.5 to 1.5
- w_query: bfloat16 [32, 2048, 2048], P('pipe', None, 'tensor'), may hold values from -0.125 to 0.125
- w_keyval: bfloat16 [32, 2048, 2, 1024], P('pipe', None, None, 'tensor'), may hold values from -0.125 to 0.125
- w_out: bfloat16 [32, 2048, 2048], P('pipe', 'tensor'), may hold values from -0.125 to 0.125
- kept_rows: int32 [32, 2, 2, 96], P('pipe', 'dp'), may hold values from 0 to 191, as said below
- doc_lengths: int32 [32, 2, 2, 4], P('pipe', 'dp'), may hold values from 1 to 96, 192 in all within a row
Outputs:
- handed: bfloat16 [32, 2, 2, 96, 2048], P('pipe', 'dp', None, 'tensor')
- back: bfloat16 [32, 2, 2, 96, 2048], P('pipe', 'dp', None, 'tensor')
- grad_query: bfloat16 [32, 2048, 2048], P('pipe', 'dp', 'tensor')
- grad_keyval: bfloat16 [32, 2048, 2, 1024], P('pipe', 'dp', None, 'tensor')
- grad_out: bfloat16 [32, 2048, 2048], P('pipe', 'tensor', 'dp')
Inputs may be any that keep to these rules, and one draw needn't show every extreme that they name: `kept_rows`: each list names 96 distinct rows in increasing order. `doc_lengths`: a list's 4 lengths sum to 192.
All inputs are finite; a program needn't handle non-finite values.
Results may differ from a plain program's by a relative error of at most 0.015.
Values may be sent and summed in bfloat16 or wider, within the bound.
A program may use at most 64 MiB of HBM per device.

v0:
```python
import jax
import jax.numpy as jnp
from jax import lax
from jax.sharding import PartitionSpec as P

HEAD = 128


EPSILON = 1e-06


def from_behind(block, axis, distance):
    devices = range(lax.axis_size(axis))
    route = [(i - distance, i) for i in devices if i - distance in devices]
    return lax.ppermute(block, axis, route)


def norm_rows(rows_in):
    widened = rows_in.astype(jnp.float32)
    inv_scale = lax.rsqrt(jnp.mean(widened * widened, axis=1, keepdims=True) + EPSILON)
    return (widened * inv_scale, inv_scale)


def doc_numbers(lengths, row_ids):
    bounds = jnp.cumsum(lengths)
    return jnp.sum((row_ids[:, None] >= bounds[None, :]).astype(jnp.int32), axis=1)


def arrange(kept_list, row_ids):
    kept_flags = jnp.any(kept_list[None, :] == row_ids[:, None], axis=1).astype(jnp.int32)
    row_order = jnp.argsort(1 - kept_flags, stable=True)
    inverse = jnp.argsort(row_order, stable=True)
    return (row_order, inverse)


def pad_rows(block, target):
    filler = jnp.zeros((target - block.shape[0],) + block.shape[1:], block.dtype)
    return jnp.concatenate([block, filler], axis=0)


def hand_over(block, step):
    return from_behind(block, "pipe", step)


def skip_over(block, step):
    return from_behind(block, "pipe", step)


def tensor_total(terms):
    return lax.psum(terms.astype(jnp.bfloat16), "tensor").astype(jnp.float32)


def heads_forward(rows_in, positions, documents, query_weight, keyval_weight):
    row_count = rows_in.shape[0]
    unrounded, inv_scale = norm_rows(rows_in)
    normed = unrounded.astype(jnp.bfloat16)
    flat_keyval = keyval_weight.reshape(keyval_weight.shape[0], -1)
    queries = jnp.dot(normed, query_weight, preferred_element_type=jnp.float32).astype(jnp.bfloat16)
    keyval = jnp.dot(normed, flat_keyval, preferred_element_type=jnp.float32).astype(jnp.bfloat16)
    groups = flat_keyval.shape[1] // (2 * HEAD)
    split_at = groups * HEAD
    queries = queries.reshape(row_count, groups, -1, HEAD)
    key_heads = keyval[:, :split_at].reshape(row_count, groups, HEAD)
    value_heads = keyval[:, split_at:].reshape(row_count, groups, HEAD)
    scores = jnp.einsum(
        "qgcd,kgd->gcqk", queries, key_heads, preferred_element_type=jnp.float32
    ) * HEAD ** (-0.5)
    allowed = (documents[:, None] == documents[None, :]) & (
        positions[None, :] <= positions[:, None]
    )
    probabilities = jax.nn.softmax(jnp.where(allowed, scores, -jnp.inf), axis=-1)
    rounded_probs = probabilities.astype(jnp.bfloat16)
    mixed_heads = jnp.einsum(
        "gcqk,kgd->qgcd", rounded_probs, value_heads, preferred_element_type=jnp.float32
    )
    mixed_heads = mixed_heads.astype(jnp.bfloat16).reshape(row_count, -1)
    return (normed, queries, key_heads, value_heads, probabilities, rounded_probs, mixed_heads)


def forward_terms(rows_in, positions, documents, query_weight, keyval_weight, out_weight):
    mixed_heads = heads_forward(rows_in, positions, documents, query_weight, keyval_weight)[-1]
    return jnp.dot(mixed_heads, out_weight, preferred_element_type=jnp.float32)


def backward_terms(
    rows_in, upstream, positions, documents, query_weight, keyval_weight, out_weight
):
    normed, queries, key_heads, value_heads, probabilities, rounded_probs, mixed_heads = (
        heads_forward(rows_in, positions, documents, query_weight, keyval_weight)
    )
    row_count = rows_in.shape[0]
    flat_keyval = keyval_weight.reshape(keyval_weight.shape[0], -1)
    contract = (((1,), (1,)), ((), ()))
    grad_mixed = lax.dot_general(upstream, out_weight, contract, preferred_element_type=jnp.float32)
    grad_mixed = grad_mixed.astype(jnp.bfloat16).reshape(queries.shape)
    grad_probs = jnp.einsum(
        "qgcd,kgd->gcqk", grad_mixed, value_heads, preferred_element_type=jnp.float32
    )
    centre = jnp.sum(probabilities * grad_probs, axis=-1, keepdims=True)
    grad_scores = (probabilities * (grad_probs - centre) * HEAD ** (-0.5)).astype(jnp.bfloat16)
    grad_query = jnp.einsum(
        "gcqk,kgd->qgcd", grad_scores, key_heads, preferred_element_type=jnp.float32
    )
    grad_query = grad_query.astype(jnp.bfloat16).reshape(row_count, -1)
    grad_keys = jnp.einsum(
        "gcqk,qgcd->kgd", grad_scores, queries, preferred_element_type=jnp.float32
    )
    grad_keys = grad_keys.astype(jnp.bfloat16).reshape(row_count, -1)
    grad_values = jnp.einsum(
        "gcqk,qgcd->kgd", rounded_probs, grad_mixed, preferred_element_type=jnp.float32
    )
    grad_values = grad_values.astype(jnp.bfloat16).reshape(row_count, -1)
    grad_keyval = jnp.concatenate([grad_keys, grad_values], axis=1)
    grad_normed = lax.dot_general(
        grad_query, query_weight, contract, preferred_element_type=jnp.float32
    )
    grad_normed = grad_normed + lax.dot_general(
        grad_keyval, flat_keyval, contract, preferred_element_type=jnp.float32
    )
    return (normed, grad_query, grad_keyval, mixed_heads, grad_normed)


def norm_back(rows_in, grad_normed, upstream):
    unrounded, inv_scale = norm_rows(rows_in)
    inner_mean = jnp.mean(grad_normed * unrounded, axis=1, keepdims=True)
    return (
        upstream.astype(jnp.float32) + inv_scale * (grad_normed - unrounded * inner_mean)
    ).astype(jnp.bfloat16)


def weight_terms(normed, grad_query, grad_keyval, mixed_heads, upstream):
    contract = (((0,), (0,)), ((), ()))
    return (
        lax.dot_general(normed, grad_query, contract, preferred_element_type=jnp.float32),
        lax.dot_general(normed, grad_keyval, contract, preferred_element_type=jnp.float32),
        lax.dot_general(mixed_heads, upstream, contract, preferred_element_type=jnp.float32),
    )


def collect(normed, grad_query, grad_keyval, mixed_heads, upstream):
    return weight_terms(normed, grad_query, grad_keyval, mixed_heads, upstream)


def local(acts_in, saved_in, out_grad, w_query, w_keyval, w_out, kept_rows, doc_lengths):
    sections = lax.axis_size("pipe")
    span_first = 0
    span_last = sections - 1
    skip_reach = span_last - span_first
    section_id = lax.axis_index("pipe")
    shard_id = lax.axis_index("tensor")
    local_rows = acts_in.shape[3]
    inputs_all, saved_all, upstream_all = (
        lax.all_gather(acts_in, "tensor", axis=3, tiled=True),
        lax.all_gather(saved_in, "tensor", axis=3, tiled=True),
        lax.all_gather(out_grad, "tensor", axis=3, tiled=True),
    )
    inputs_all = inputs_all[0, 0]
    saved_all = saved_all[0, 0]
    upstream_all = upstream_all[0, 0]
    keep_count = inputs_all.shape[1]
    total_rows = 2 * keep_count
    model_width = inputs_all.shape[2]
    row_ids = jnp.arange(total_rows, dtype=jnp.int32)
    query_weight = w_query[0]
    keyval_weight = w_keyval[0]
    out_weight = w_out[0]
    kept_mode = (section_id >= span_first) & (section_id < span_last)
    at_first = section_id == span_first
    at_last = section_id == span_last
    zero_slab = jnp.zeros((local_rows, model_width), jnp.bfloat16)

    def own_slab(block):
        return lax.dynamic_slice_in_dim(block, shard_id * local_rows, local_rows, 0)

    kept_fwd = kept_rows[0, 0, 0]
    docs_fwd = doc_numbers(doc_lengths[0, 0, 0], row_ids)
    order_fwd, inverse_fwd = arrange(kept_fwd, row_ids)
    straight = inputs_all.reshape(total_rows, model_width)
    full_rows = jnp.where(at_last, jnp.take(straight, inverse_fwd, axis=0), straight)
    picked = jnp.where(at_first, jnp.take(full_rows, kept_fwd, axis=0), inputs_all[0])
    picked_docs = jnp.take(docs_fwd, kept_fwd)

    def forward_kept(operand):
        terms = forward_terms(
            operand[0], kept_fwd, picked_docs, query_weight, keyval_weight, out_weight
        )
        return pad_rows(terms, total_rows)

    def forward_full(operand):
        return forward_terms(operand[1], row_ids, docs_fwd, query_weight, keyval_weight, out_weight)

    partial_value = lax.cond(kept_mode, forward_kept, forward_full, (picked, full_rows))
    summed = tensor_total(partial_value)
    full_out = (full_rows.astype(jnp.float32) + summed).astype(jnp.bfloat16)
    kept_out = (picked.astype(jnp.float32) + summed[:keep_count]).astype(jnp.bfloat16)
    full_buf = jnp.stack([own_slab(full_out[:keep_count]), own_slab(full_out[keep_count:])])
    kept_buf = jnp.stack([own_slab(kept_out), zero_slab])
    out_buf = jnp.where(kept_mode, kept_buf, full_buf)
    drop_share = own_slab(jnp.take(full_rows, order_fwd[keep_count:], axis=0))
    handed = hand_over(out_buf, 1)
    arrived = skip_over(drop_share, skip_reach)
    handed = jnp.where(at_last, jnp.stack([handed[0], arrived]), handed)
    kept_back = kept_rows[0, 0, 1]
    docs_back = doc_numbers(doc_lengths[0, 0, 1], row_ids)
    order_back, inverse_back = arrange(kept_back, row_ids)
    saved_straight = saved_all.reshape(total_rows, model_width)
    saved_full = jnp.where(at_last, jnp.take(saved_straight, inverse_back, axis=0), saved_straight)
    saved_kept = jnp.where(at_first, jnp.take(saved_full, kept_back, axis=0), saved_all[0])
    upstream_full = upstream_all.reshape(total_rows, model_width)
    upstream_kept = upstream_all[0]
    back_docs = jnp.take(docs_back, kept_back)

    def backward_kept(operand):
        normed, grad_query, grad_keyval, mixed_heads, grad_normed = backward_terms(
            operand[0], operand[1], kept_back, back_docs, query_weight, keyval_weight, out_weight
        )
        return (
            pad_rows(grad_normed, total_rows),
            collect(normed, grad_query, grad_keyval, mixed_heads, operand[1]),
        )

    def backward_full(operand):
        normed, grad_query, grad_keyval, mixed_heads, grad_normed = backward_terms(
            operand[2], operand[3], row_ids, docs_back, query_weight, keyval_weight, out_weight
        )
        return (grad_normed, collect(normed, grad_query, grad_keyval, mixed_heads, operand[3]))

    grad_partial, collected = lax.cond(
        kept_mode,
        backward_kept,
        backward_full,
        (saved_kept, upstream_kept, saved_full, upstream_full),
    )
    grad_summed = tensor_total(grad_partial)
    full_grad = norm_back(saved_full, grad_summed, upstream_full)
    kept_grad = norm_back(saved_kept, grad_summed[:keep_count], upstream_kept)
    plain_buf = jnp.stack([own_slab(full_grad[:keep_count]), own_slab(full_grad[keep_count:])])
    last_buf = jnp.stack([own_slab(jnp.take(full_grad, kept_back, axis=0)), zero_slab])
    joined = jnp.take(jnp.concatenate([kept_grad, upstream_all[1]], axis=0), inverse_back, axis=0)
    first_buf = jnp.stack([own_slab(joined[:keep_count]), own_slab(joined[keep_count:])])
    inner_buf = jnp.stack([own_slab(kept_grad), zero_slab])
    back_buf = jnp.where(
        at_first,
        first_buf,
        jnp.where(kept_mode, inner_buf, jnp.where(at_last, last_buf, plain_buf)),
    )
    drop_back = own_slab(jnp.take(full_grad, order_back[keep_count:], axis=0))
    returned = hand_over(back_buf, -1)
    came_back = skip_over(drop_back, -skip_reach)
    returned = jnp.where(at_first, jnp.stack([returned[0], came_back]), returned)
    grad_q_local, grad_kv_local, grad_o_local = collected
    grad_kv_local = grad_kv_local.reshape(grad_kv_local.shape[0], 2, -1)
    summed_query, summed_keyval, summed_out = (
        lax.psum_scatter(
            grad_q_local.astype(jnp.bfloat16), "dp", scatter_dimension=0, tiled=True
        ).astype(jnp.float32),
        lax.psum_scatter(
            grad_kv_local.astype(jnp.bfloat16), "dp", scatter_dimension=0, tiled=True
        ).astype(jnp.float32),
        lax.psum_scatter(
            grad_o_local.astype(jnp.bfloat16), "dp", scatter_dimension=1, tiled=True
        ).astype(jnp.float32),
    )
    return (
        handed[None, None],
        returned[None, None],
        summed_query.astype(jnp.bfloat16)[None],
        summed_keyval.astype(jnp.bfloat16)[None],
        summed_out.astype(jnp.bfloat16)[None],
    )


def solution(mesh):
    placed = (
        P("pipe", "dp", None, "tensor", None),
        P("pipe", "dp", None, "tensor", None),
        P("pipe", "dp", None, "tensor", None),
        P("pipe", None, "tensor"),
        P("pipe", None, None, "tensor"),
        P("pipe", "tensor", None),
        P("pipe", "dp", None, None),
        P("pipe", "dp", None, None),
    )
    return jax.shard_map(
        local,
        mesh=mesh,
        in_specs=placed,
        out_specs=(
            P("pipe", "dp", None, "tensor", None),
            P("pipe", "dp", None, "tensor", None),
            P("pipe", "dp", "tensor"),
            P("pipe", "dp", None, "tensor"),
            P("pipe", "tensor", "dp"),
        ),
        check_vma=False,
    )
```

profile of v0, /device:TPU:1, one launch (start us, length us, event | category | flops | bytes accessed | tf_op | source)
XLA Modules:
  0.0 471.7 jit_solution(14229057206504444818)
XLA Ops:
  7.2 1.3 fusion.166
  8.7 3.2 sort.61
  11.9 3.2 sort.62
  15.1 1.3 compare_and_fusion.6
  16.4 3.2 sort.59
  19.6 3.2 sort.60
  22.8 20.4 %all_gather.11 = bf16[1,1,2,96,2048]{4,2,1,0,3:T(2,128)(2,1)S(1)} all-gather(bf16[1,1,2,12,2048]{4,2,1,0,3:T(2,128)(2,1)} %bitcast.392), channel_id=1, replica_groups=mesh['pipe'=32,'dp'=2,'tensor'=8] {'tensor'}, dimensions={3}, use_global_device_ids=true | all-gather | bytes 884736 | tf_op jit(solution)/shard_map/all_gather | solution.py:154
  43.8 1.1 gather_fusion.4
  45.2 1.6 gather_fusion.5
  46.8 1.8 gather_fusion.6
  48.6 13.5 %all_gather.10 = bf16[1,1,2,96,2048]{4,2,1,0,3:T(2,128)(2,1)S(1)} all-gather(bf16[1,1,2,12,2048]{4,2,1,0,3:T(2,128)(2,1)S(1)} %bitcast.393), channel_id=1, replica_groups=mesh['pipe'=32,'dp'=2,'tensor'=8] {'tensor'}, dimensions={3}, use_global_device_ids=true | all-gather | bytes 884736 | tf_op jit(solution)/shard_map/all_gather | solution.py:155
  62.3 1.0 slice_bitcast_fusion.20
  63.3 13.5 %all_gather.9 = bf16[1,1,2,96,2048]{4,2,1,0,3:T(2,128)(2,1)S(1)} all-gather(bf16[1,1,2,12,2048]{4,2,1,0,3:T(2,128)(2,1)S(1)} %bitcast.394), channel_id=1, replica_groups=mesh['pipe'=32,'dp'=2,'tensor'=8] {'tensor'}, dimensions={3}, use_global_device_ids=true | all-gather | bytes 884736 | tf_op jit(solution)/shard_map/all_gather | solution.py:153
  77.4 2.0 gather_fusion
  79.4 1.3 select_select_fusion.1
  80.7 1.6 gather_fusion.1
  82.3 1.7 gather_fusion.2
  84.6 1.9 fusion.147
  86.5 1.9 fusion.149
  88.5 7.1 %conditional.3 = (bf16[192,2048]{1,0:T(8,128)(2,1)S(1)}, bf16[2048,256]{1,0:T(8,128)(2,1)S(1)}, bf16[2048,256]{1,0:T(8,128)(2,1)S(1)}, bf16[256,2048]{1,0:T(8,128)(2,1)S(1)}) conditional(s32[]{:T(128)} %convert_element_type.240, (bf16[192,2048]{1,0:T(8,128)(2,1)S(1)}, bf16[1,2048,2,128]{3,2,1,0:T(2,128)(2,1)}, s32[192]{0:T(256)S(1)}, ...), branch_computations={%region_20.28_spmd, %region_25.33_spmd} | conditional | flops 1732889600 | bytes 31441240 | solution.py:228
  88.9 1.7 convolution_convert_fusion.13
  97.5 4.3 conditional.2
  97.7 1.6 convolution_convert_fusion.4
  100.8 1.0 concatenate.10
  101.8 1.1 copy-done.20
  103.0 1.1 convert_element_type.259
  106.7 12.5 %collective-permute-start.1 = (bf16[12,2048]{1,0:T(8,128)(2,1)}, bf16[12,2048]{1,0:T(8,128)(2,1)}, u32[]{:S(2)}, u32[]{:S(2)}) collective-permute-start(bf16[12,2048]{1,0:T(8,128)(2,1)} %dynamic-slice_select_fusion.2), channel_id=1, source_target_pairs={{0,496},{1,497},{2,498},{3,499},{4,500},{5,501},{6,502},{7,503},{8... | collective-permute-start | bytes 147464 | tf_op jit(solution)/shard_map/ppermute | solution.py:15
  121.9 1.3 dynamic-slice
  123.9 54.3 %all-reduce.12.cloned.1.call-done = (bf16[192,2048]{1,0:T(8,128)(2,1)}, bf16[192,2048]{1,0:T(8,128)(2,1)}) async-done(((bf16[192,2048]{1,0:T(8,128)(2,1)}, bf16[192,2048]{1,0:T(8,128)(2,1)}), (bf16[192,2048]{1,0:T(8,128)(2,1)}, bf16[192,2048]{1,0:T(8,128)(2,1)})) %all-reduce.12.cloned.1.call-update) | async-done | bytes 1572880 | tf_op jit(solution)/shard_map/psum | solution.py:50
  178.2 1.6 fusion.134
  181.3 1.6 gather_fusion.8
  183.1 1.0 copy-done.16
  184.0 0.9 slice.137
  185.2 1.5 dynamic-slice_bitcast_fusion.2
  186.8 1.5 dynamic-slice_bitcast_fusion.1
  189.4 1.1 gather_fusion.7
  191.2 1.0 fusion.157
  192.3 1.3 collective-permute-start.2
  193.6 1.0 gather_fusion.9
  194.7 1.3 collective-permute-start.3
  196.0 1.0 fusion.156
  197.2 3.4 collective-permute-start
  200.6 8.3 %collective-permute-done.3 = bf16[12,2048]{1,0:T(8,128)(2,1)S(1)} collective-permute-done((bf16[12,2048]{1,0:T(8,128)(2,1)S(1)}, bf16[12,2048]{1,0:T(8,128)(2,1)S(1)}, u32[]{:S(2)}, u32[]{:S(2)}) %collective-permute-start.3) | collective-permute-done | bytes 49184 | tf_op jit(solution)/shard_map/ppermute | solution.py:15
  209.7 1.8 collective-permute-done
  213.1 113.8 %all-reduce.10.cloned.1.call-done = bf16[2048,2,128]{2,1,0:T(2,128)(2,1)} async-done(((bf16[2048,2,128]{2,1,0:T(2,128)(2,1)}), bf16[2048,2,128]{2,1,0:T(2,128)(2,1)}) %all-reduce.10.cloned.1.call-update) | async-done | bytes 1048592
  326.9 2.2 dynamic-slice_bitcast_fusion
  329.1 67.1 %reduce-scatter.3.cloned.1.call-done = bf16[1024,256]{1,0:T(8,128)(2,1)} async-done(((bf16[2048,256]{1,0:T(8,128)(2,1)}), bf16[1024,256]{1,0:T(8,128)(2,1)}) %reduce-scatter.3.cloned.1.call-update) | async-done | bytes 524304 | tf_op jit(solution)/shard_map/reduce_scatter | solution.py:254
  396.2 69.0 %reduce-scatter.5.cloned.1.call-done = bf16[256,1024]{1,0:T(8,128)(2,1)} async-done(((bf16[256,2048]{1,0:T(8,128)(2,1)}), bf16[256,1024]{1,0:T(8,128)(2,1)}) %reduce-scatter.5.cloned.1.call-update) | async-done | bytes 524304 | tf_op jit(solution)/shard_map/reduce_scatter | solution.py:260
  (186 shorter events, 22.5 us)
Async XLA Ops:
  7.2 36.3 %copy-start.37 = (s32[1,1,2,4]{3,2,1,0:T(2,128)S(1)}, s32[1,1,2,4]{3,2,1,0:T(2,128)}, u32[]{:S(2)}) copy-start(s32[1,1,2,4]{3,2,1,0:T(2,128)} %param.25) | copy-start | bytes 100
  7.2 171.0 %all-reduce.12.cloned.1.call-start = ((), (), s32[]{:S(2)}) async-start(), calls=%async_computation.5 | async-start | bytes 3145728 | tf_op jit(solution)/shard_map/psum | solution.py:50
  11.9 3.2 copy-start.38
  15.1 29.8 %copy-start.35 = (pred[192]{0:T(512)(128)(4,1)}, pred[192]{0:T(512)(128)(4,1)S(1)}, u32[]{:S(2)}) copy-start(pred[192]{0:T(512)(128)(4,1)S(1)} %compare_and_fusion.5) | copy-start | bytes 580
  19.6 25.3 %copy-start.40 = (s32[192]{0:T(256)}, s32[192]{0:T(256)S(1)}, u32[]{:S(2)}) copy-start(s32[192]{0:T(256)S(1)} %get-tuple-element.97) | copy-start | bytes 2308
  45.2 3.4 copy-start.24
  62.0 1.3 copy-start.25
  62.3 14.8 %copy-start = (bf16[1,1,2,96,2048]{4,3,2,1,0:T(8,128)(2,1)}, bf16[1,1,2,96,2048]{4,3,2,1,0:T(8,128)(2,1)S(1)}, u32[]{:S(2)}) copy-start(bf16[1,1,2,96,2048]{4,3,2,1,0:T(8,128)(2,1)S(1)} %copy.121) | copy-start | bytes 2359300
  84.0 4.4 copy-start.1
  84.0 4.4 copy-start.3
  84.0 4.4 copy-start.15
  84.0 4.4 copy-start.26
  84.0 4.4 copy-start.30
  84.0 4.4 copy-start.34
  88.4 7.2 %copy-start.4 = (bf16[1,2048,256]{2,1,0:T(8,128)(2,1)S(1)}, bf16[1,2048,256]{2,1,0:T(8,128)(2,1)}, u32[]{:S(2)}) copy-start(bf16[1,2048,256]{2,1,0:T(8,128)(2,1)} %param.21) | copy-start | bytes 3145732
  88.4 7.2 %copy-start.14 = (bf16[96,2048]{1,0:T(8,128)(2,1)S(1)}, bf16[96,2048]{1,0:T(8,128)(2,1)}, u32[]{:S(2)}) copy-start(bf16[96,2048]{1,0:T(8,128)(2,1)} %fusion.149) | copy-start | bytes 1179652
  88.5 7.2 %copy-start.28 = (pred[96]{0:T(512)(128)(4,1)S(1)}, pred[96]{0:T(512)(128)(4,1)}, u32[]{:S(2)}) copy-start(pred[96]{0:T(512)(128)(4,1)} %get-tuple-element.169) | copy-start | bytes 292
  88.5 7.2 %copy-start.29 = (s32[1,1,1,96]{3,2,1,0:T(1,128)S(1)}, s32[1,1,1,96]{3,2,1,0:T(1,128)}, u32[]{:S(2)}) copy-start(s32[1,1,1,96]{3,2,1,0:T(1,128)} %get-tuple-element.168) | copy-start | bytes 1156
  88.9 2.4 copy-start.6
  92.0 1.2 copy-start.12
  95.6 1.0 copy-start.13
  95.6 1.2 copy-start.17
  95.6 1.6 copy-start.19
  95.6 1.9 copy-start.21
  97.7 2.0 copy-start.33
  99.3 1.2 copy-start.8
  101.8 1.2 copy-start.20
  101.8 225.1 %all-reduce.10.cloned.1.call-start = ((), (), s32[]{:S(2)}) async-start(), calls=%async_computation.4 | async-start | bytes 2097152
  104.1 0.8 copy-start.41
  104.1 292.1 %reduce-scatter.3.cloned.1.call-start = ((), (), s32[]{:S(2)}) async-start(), calls=%async_computation.2 | async-start | bytes 1572864 | tf_op jit(solution)/shard_map/reduce_scatter | solution.py:254
  104.9 360.3 %reduce-scatter.5.cloned.1.call-start = ((), (), s32[]{:S(2)}) async-start(), calls=%async_computation.3 | async-start | bytes 1572864 | tf_op jit(solution)/shard_map/reduce_scatter | solution.py:260
  105.9 13.6 %copy-start.27 = (pred[96]{0:T(512)(128)(4,1)S(1)}, pred[96]{0:T(512)(128)(4,1)}, u32[]{:S(2)}) copy-start(pred[96]{0:T(512)(128)(4,1)} %get-tuple-element.141) | copy-start | bytes 292
  105.9 14.3 %copy-start.39 = (s32[192]{0:T(256)S(1)}, s32[192]{0:T(256)}, u32[]{:S(2)}) copy-start(s32[192]{0:T(256)} %copy-done.38) | copy-start | bytes 2308
  105.9 14.4 %copy-start.42 = (f32[96]{0:T(128)S(1)}, f32[96]{0:T(128)}, u32[]{:S(2)}) copy-start(f32[96]{0:T(128)} %get-tuple-element.137) | copy-start | bytes 1156
  106.7 104.8 %collective-permute-start.1 = (bf16[12,2048]{1,0:T(8,128)(2,1)}, bf16[12,2048]{1,0:T(8,128)(2,1)}, u32[]{:S(2)}, u32[]{:S(2)}) collective-permute-start(bf16[12,2048]{1,0:T(8,128)(2,1)} %dynamic-slice_select_fusion.2), channel_id=1, source_target_pairs={{0,496},{1,497},{2,498},{3,499},{4,500},{5,501},{6,502},{7,503},{8... | collective-permute-start | bytes 147464 | tf_op jit(solution)/shard_map/ppermute | solution.py:15
  119.2 60.6 %copy-start.2 = (bf16[1,1,2,96,2048]{4,3,2,1,0:T(8,128)(2,1)S(1)}, bf16[1,1,2,96,2048]{4,3,2,1,0:T(8,128)(2,1)}, u32[]{:S(2)}) copy-start(bf16[1,1,2,96,2048]{4,3,2,1,0:T(8,128)(2,1)} %copy-done) | copy-start | bytes 2359300
  178.2 1.6 copy-start.9
  181.3 1.6 copy-start.10
  182.9 1.1 copy-start.16
  185.0 3.4 copy-start.32
  188.3 1.0 copy-start.18
  189.4 1.2 copy-start.36
  190.6 1.6 copy-start.22
  190.6 1.6 copy-start.23
  192.3 2.3 copy-start.43
  192.3 8.2 %collective-permute-start.2 = (bf16[2,12,2048]{2,1,0:T(8,128)(2,1)S(1)}, bf16[2,12,2048]{2,1,0:T(8,128)(2,1)S(1)}, u32[]{:S(2)}, u32[]{:S(2)}) collective-permute-start(bf16[2,12,2048]{2,1,0:T(8,128)(2,1)S(1)} %maximum_select_fusion.2), channel_id=1, source_target_pairs={{16,0},{32,16},{48,32},{64,48},{80,64},{96,80},{112,96},{128,112},... | collective-permute-start | bytes 294920 | tf_op jit(solution)/shard_map/ppermute | solution.py:15
  194.7 14.2 %collective-permute-start.3 = (bf16[12,2048]{1,0:T(8,128)(2,1)S(1)}, bf16[12,2048]{1,0:T(8,128)(2,1)S(1)}, u32[]{:S(2)}, u32[]{:S(2)}) collective-permute-start(bf16[12,2048]{1,0:T(8,128)(2,1)S(1)} %dynamic-slice_select_fusion), channel_id=1, source_target_pairs={{496,0},{497,1},{498,2},{499,3},{500,4},{501,5},{502,6},{503,7},{5... | collective-permute-start | bytes 147464 | tf_op jit(solution)/shard_map/ppermute | solution.py:15
  197.2 14.3 %collective-permute-start = (bf16[2,12,2048]{2,1,0:T(8,128)(2,1)S(1)}, bf16[2,12,2048]{2,1,0:T(8,128)(2,1)S(1)}, u32[]{:S(2)}, u32[]{:S(2)}) collective-permute-start(bf16[2,12,2048]{2,1,0:T(8,128)(2,1)S(1)} %maximum_select_fusion), channel_id=1, source_target_pairs={{0,16},{16,32},{32,48},{48,64},{64,80},{80,96},{96,112},{112,128},... | collective-permute-start | bytes 294920 | tf_op jit(solution)/shard_map/ppermute | solution.py:15
  (1 other events, 0.7 us)
Sparse Core Ops, SparseCore 0:
  101.9 76.2 all-reduce.11
  181.1 145.7 all-reduce.9
  330.5 65.6 reduce-scatter.2
  399.4 65.6 reduce-scatter.4
where the time goes:
time: 473 us; the launch traced here: 472 us
  waiting for transfers between devices  315 us (67%)
  blocking collectives  47.3 us (10%)
  local copies, waits for them, and re-layouts  36.9 us (8%)
  other arithmetic  29.5 us (6%)
  starting transfers between devices  18.6 us (4%)
  between operations  15.1 us (3%)
  matrix products  8.86 us (2%)
    unnamed x5, waiting for transfers between devices  115 us
    reduce_scatter x1, waiting for transfers between devices, local(): lax.psum_scatter(grad_o_local.astype(jnp.bfloat16), 'dp', scatter_dimensi...  69 us
    reduce_scatter x1, waiting for transfers between devices, local(): lax.psum_scatter(grad_q_local.astype(jnp.bfloat16), 'dp', scatter_dimensi...  67.1 us
    psum x1, waiting for transfers between devices, tensor_total(): return lax.psum(terms.astype(jnp.bfloat16), 'tensor').astype(jnp.float32)  54.3 us
    all_gather x1, blocking collectives, local(): lax.all_gather(saved_in, 'tensor', axis=3, tiled=True)  20.4 us
    ppermute x4, starting transfers between devices, from_behind(): return lax.ppermute(block, axis, route)  18.5 us
    all_gather x1, blocking collectives, local(): lax.all_gather(acts_in, 'tensor', axis=3, tiled=True)  13.5 us
    all_gather x1, blocking collectives, local(): lax.all_gather(out_grad, 'tensor', axis=3, tiled=True)  13.5 us
  transfers between devices with their start and end apart: 8, of which 6 were waited for; matrix products, arithmetic and copies ran while one was open for 5% of the time, Pallas kernels for 0%

commit v1 on v0

v1 whole, which is shorter than its diff:
```python
import jax
import jax.numpy as jnp
from jax import lax
from jax.experimental import pallas as pl
from jax.experimental.pallas import tpu as pltpu
from jax.sharding import PartitionSpec as P

HEAD = 128
EPSILON = 1e-06
MESH = pl.DeviceIdType.MESH
F32 = jnp.float32
BF16 = jnp.bfloat16

SAVED, GRAD, ACTS, SAVED_2, GRAD_2 = range(5)
BACK, FORWARD = 0, 1
ROWS_PAD = 16
SLABS = 8
HALF_ROWS = SLABS * ROWS_PAD


def nn(a, b):
    return lax.dot_general(a, b, (((1,), (0,)), ((), ())), preferred_element_type=F32)


def nt(a, b):
    return lax.dot_general(a, b, (((1,), (1,)), ((), ())), preferred_element_type=F32)


def tn(a, b):
    return lax.dot_general(a, b, (((0,), (0,)), ((), ())), preferred_element_type=F32)


def iota(shape, dim):
    return lax.broadcasted_iota(jnp.int32, shape, dim)


def list_index(a, real_rows):
    core, y, r = a // 64, (a // 16) % 4, a % 16
    return (2 * y + core) * real_rows + r, r < real_rows


def to_row(col):
    n = col.shape[0]
    return jnp.sum(jnp.where(iota((n, n), 0) == iota((n, n), 1), col, 0.0), axis=0, keepdims=True)


def to_col(row):
    n = row.shape[1]
    return jnp.sum(jnp.where(iota((n, n), 0) == iota((n, n), 1), row, 0.0), axis=1, keepdims=True)


def kept_positions(kept, real_rows):
    keep = kept.shape[1]
    place, real = list_index(iota((HALF_ROWS, keep), 0), real_rows)
    hit = (place == iota((HALF_ROWS, keep), 1)) & real
    found = jnp.sum(jnp.where(hit, kept, 0.0), axis=1, keepdims=True)
    _, real_col = list_index(iota((HALF_ROWS, 1), 0), real_rows)
    return jnp.where(real_col, found, 1000.0)


def dropped_positions(kept, real_rows):
    keep = kept.shape[1]
    n = 256
    named = jnp.max(
        jnp.where(iota((n, keep), 0).astype(F32) == kept, 1.0, 0.0), axis=1, keepdims=True
    )
    free = jnp.where(iota((n, 1), 0) < 2 * keep, 1.0 - named, 0.0)
    count = jnp.sum(
        jnp.where(iota((n, n), 1) <= iota((n, n), 0), to_row(free), 0.0), axis=1, keepdims=True
    )
    place, real = list_index(iota((n, HALF_ROWS), 1), real_rows)
    hit = (count - 1.0 == place.astype(F32)) & (free > 0.5) & real
    found = jnp.sum(jnp.where(hit, iota((n, HALF_ROWS), 0).astype(F32), 0.0), axis=0, keepdims=True)
    _, real_row = list_index(iota((1, HALF_ROWS), 1), real_rows)
    return jnp.where(real_row, found, 1000.0)


def document_of(positions, lengths):
    bound = jnp.zeros((1, 1), F32)
    total = jnp.zeros(positions.shape, F32)
    for m in range(lengths.shape[1]):
        bound = bound + lengths[:, m : m + 1]
        total = total + jnp.where(positions >= bound, 1.0, 0.0)
    return total


def select(pos_col, real_rows, keep):
    n = 2 * HALF_ROWS
    b = iota((1, n), 1)
    place, real = list_index(b % HALF_ROWS, real_rows)
    flat = jnp.where(real, (b // HALF_ROWS) * keep + place, -1).astype(F32)
    return jnp.where(pos_col == flat, 1.0, 0.0).astype(BF16)


def inverse_root(x):
    return lax.rsqrt(jnp.mean(x * x, axis=1, keepdims=True) + EPSILON)


def kernel(
    acts, saved, ograd, kept, lens, wq_hbm, wkv_hbm, wo_hbm,
    handed, back, gq_out, gkv_out, go_out,
    buf, wq, wkv, wo, kept2, lens2, normed, picked, gpick, stash, part, sibrecv, chip, yrecv, hsrc, hrecv,
    wsem, dps, dpr, ags, agr, r1s, r1r, r2s, r2r, hs, hr,
):
    pipes = lax.axis_size("pipe")
    p, r, t = lax.axis_index("pipe"), lax.axis_index("dp"), lax.axis_index("tensor")
    y, c = t // 2, t % 2
    own = c * 4 + y
    first, last = p == 0, p == pipes - 1
    edge = first | last
    inner = jnp.logical_not(edge)
    real_rows, width = acts.shape[3], acts.shape[4]
    keep = kept.shape[3]
    half_width = width // 2
    next_pipe = {"pipe": lax.rem(p + 1, pipes)}
    prev_pipe = {"pipe": lax.rem(p + pipes - 1, pipes)}
    sibling = {"tensor": y * 2 + 1 - c}
    other_dp = {"dp": 1 - r}

    def peer_y(d):
        return lax.rem(y + d, 4)

    def remote(src, dst, send, recv, device):
        return pltpu.make_async_remote_copy(
            src_ref=src, dst_ref=dst, send_sem=send, recv_sem=recv, device_id=device, device_id_type=MESH
        )

    def slots_of(arr, action):
        action(arr, 0)
        used = last if arr in (GRAD, GRAD_2) else edge

        @pl.when(used)
        def _():
            action(arr, 1)

    loads = [
        pltpu.make_async_copy(src.at[0] if src is not wkv_hbm else src, dst, wsem.at[i])
        for i, (src, dst) in enumerate(((wq_hbm, wq), (wkv_hbm, wkv), (wo_hbm, wo)))
    ]
    for load in loads:
        load.start()

    barrier = pltpu.get_barrier_semaphore()
    greet = [{"tensor": lax.rem(t + d, 8)} for d in range(1, 8)] + [other_dp, next_pipe, prev_pipe]
    for device in greet:
        pl.semaphore_signal(barrier, inc=1, device_id=device, device_id_type=MESH)

    filler = jnp.zeros((ROWS_PAD - real_rows, width), BF16)
    for arr, src in ((SAVED, saved), (GRAD, ograd), (ACTS, acts)):
        for slot in range(2):
            buf[arr, slot, own, 0:real_rows, :] = src[0, 0, slot]
            buf[arr, slot, own, real_rows:, :] = filler

    pl.semaphore_wait(barrier, len(greet))

    def dp_copy(arr, slot):
        return remote(
            buf.at[arr, slot, own], buf.at[arr + 3, slot, own],
            dps.at[arr, slot], dpr.at[arr, slot], other_dp,
        )

    kept_copy = remote(kept.at[0, 0], kept2, dps.at[2, 0], dpr.at[2, 0], other_dp)
    lens_copy = remote(lens.at[0, 0], lens2, dps.at[2, 1], dpr.at[2, 1], other_dp)
    slots_of(SAVED, lambda arr, slot: dp_copy(arr, slot).start())
    slots_of(GRAD, lambda arr, slot: dp_copy(arr, slot).start())
    kept_copy.start()
    lens_copy.start()

    def slab_to(arr, slot, slab, sem, device):
        here = buf.at[arr, slot, slab]
        return remote(here, here, ags.at[arr, slot, sem], agr.at[arr, slot, slab], device)

    def ag_start(arr, slot):
        for d in (2, 1, 3):
            slab_to(arr, slot, own, d - 1, {"tensor": peer_y(d) * 2 + c}).start()
        slab_to(arr, slot, own, 3, sibling).start()

    def ag_pass(arr, slot):
        for d in (1, 3, 2):
            slab = c * 4 + peer_y(d)
            copy = slab_to(arr, slot, slab, 3 + d, sibling)
            copy.wait_recv()
            copy.start()

    def ag_wait(arr, slot):
        for d in range(4):
            slab_to(arr, slot, (1 - c) * 4 + peer_y(d), 3, sibling).wait_recv()

    def ag_end(arr, slot):
        for d in range(7):
            slab_to(arr, slot, own, d, sibling).wait_send()

    for arr in (SAVED, GRAD, ACTS):
        slots_of(arr, ag_start)

    kept_back = kept[0, 0, 1:2, :].astype(F32)
    lens_back = lens[0, 0, 1:2, :].astype(F32)
    kept_fwd = kept[0, 0, 0:1, :].astype(F32)
    lens_fwd = lens[0, 0, 0:1, :].astype(F32)

    for load in loads:
        load.wait()

    for arr in (SAVED, GRAD):
        slots_of(arr, ag_pass)
    for arr in (SAVED, GRAD):

        def relay(arr, slot):
            dp_copy(arr, slot).wait_recv()
            ag_start(arr + 3, slot)

        slots_of(arr, relay)
    slots_of(ACTS, ag_pass)

    def rows_of(arr, slot):
        return buf[arr, slot].reshape(HALF_ROWS, width)

    def normalise(which, slab_of, slabs):
        def step(i, carry):
            x = slab_of(i).astype(F32)
            normed[which, pl.ds(pl.multiple_of(i * ROWS_PAD, ROWS_PAD), ROWS_PAD), :] = (
                x * inverse_root(x)
            ).astype(BF16)
            return carry

        lax.fori_loop(0, slabs, step, 0)

    def pick(arr, pos_col, into):
        chosen = select(pos_col, real_rows, keep)
        for n0 in range(0, width, 512):
            cols = slice(n0, n0 + 512)
            got = nn(chosen[:, :HALF_ROWS], buf[arr, 0, :, :, cols].reshape(HALF_ROWS, 512))
            got = got + nn(chosen[:, HALF_ROWS:], buf[arr, 1, :, :, cols].reshape(HALF_ROWS, 512))
            into[:, cols] = got.astype(BF16)

    def prepare(arr, which, kept_list):
        @pl.when(inner)
        def _():
            normalise(which, lambda i: buf[arr, 0, i], SLABS)

        @pl.when(first)
        def _():
            pick(arr, kept_positions(kept_list, real_rows), picked.at[which])
            normalise(
                which,
                lambda i: picked[which, pl.ds(pl.multiple_of(i * ROWS_PAD, ROWS_PAD), ROWS_PAD), :],
                SLABS,
            )

        @pl.when(last)
        def _():
            normalise(which, lambda i: buf[arr, i // SLABS, i % SLABS], 2 * SLABS)

    def places(kept_list, lengths, rows):
        pos_col = kept_positions(kept_list, real_rows)
        pos_row = to_row(pos_col)
        if rows > HALF_ROWS:
            more = dropped_positions(kept_list, real_rows)
            pos_row = jnp.concatenate([pos_row, more], axis=1)
            pos_col = jnp.concatenate([pos_col, to_col(more)], axis=0)
        allowed = (document_of(pos_col, lengths) == document_of(pos_row, lengths)) & (
            pos_row <= pos_col
        )
        return pos_col, allowed

    def heads(which, rows, allowed):
        x = normed[which, 0:rows, :]
        queries = nn(x, wq[...]).astype(BF16)
        keyval = nn(x, wkv[...]).astype(BF16)
        keys, values = keyval[:, :HEAD], keyval[:, HEAD:]
        out = []
        for h in range(2):
            q = queries[:, h * HEAD : (h + 1) * HEAD]
            scores = jnp.where(allowed, nt(q, keys) * HEAD ** (-0.5), -jnp.inf)
            e = jnp.exp(scores - jnp.max(scores, axis=1, keepdims=True))
            probs = e / jnp.sum(e, axis=1, keepdims=True)
            rounded = probs.astype(BF16)
            out.append((q, probs, rounded, nn(rounded, values).astype(BF16)))
        return keys, values, out

    def run_forward(rows):
        _, allowed = places(kept_fwd, lens_fwd, rows)
        _, _, out = heads(2, rows, allowed)
        mixed = jnp.concatenate([o[3] for o in out], axis=1)
        for n0 in range(0, width, 512):
            store_part(FORWARD, rows, n0, nn(mixed, wo[:, n0 : n0 + 512]))

    def store_part(f, rows, n0, value):
        value = value.astype(BF16)
        for slot in range(rows // HALF_ROWS):
            part[f, slot, :, :, n0 : n0 + 512] = value[
                slot * HALF_ROWS : (slot + 1) * HALF_ROWS
            ].reshape(SLABS, ROWS_PAD, 512)

    def cotangent(which, rows, pos_col):
        arr = GRAD + 3 * which
        if rows > HALF_ROWS:
            pick(arr, pos_col, gpick.at[which])
            return gpick[which]
        return rows_of(arr, 0)

    def run_back(which, rows, kept_list, lengths):
        pos_col, allowed = places(kept_list, lengths, rows)
        upstream = cotangent(which, rows, pos_col)
        grad_mixed = nt(upstream, wo[...]).astype(BF16)
        keys, values, out = heads(which, rows, allowed)
        grad_k = jnp.zeros((rows, HEAD), F32)
        grad_v = jnp.zeros((rows, HEAD), F32)
        grad_q = []
        for h, (q, probs, rounded, _) in enumerate(out):
            gm = grad_mixed[:, h * HEAD : (h + 1) * HEAD]
            grad_probs = nt(gm, values)
            centre = jnp.sum(probs * grad_probs, axis=1, keepdims=True)
            scores = (probs * (grad_probs - centre) * HEAD ** (-0.5)).astype(BF16)
            grad_q.append(nn(scores, keys).astype(BF16))
            grad_k = grad_k + tn(scores, q)
            grad_v = grad_v + tn(rounded, gm)
        gq = jnp.concatenate(grad_q, axis=1)
        gkv = jnp.concatenate([grad_k.astype(BF16), grad_v.astype(BF16)], axis=1)
        stash[which, 0, 0:rows, :] = gq
        stash[which, 1, 0:rows, :] = gkv
        stash[which, 2, 0:rows, :] = jnp.concatenate([o[3] for o in out], axis=1)
        if which == 0:
            for n0 in range(0, width, 512):
                term = nt(gq, wq[n0 : n0 + 512, :]) + nt(gkv, wkv[n0 : n0 + 512, :])
                store_part(BACK, rows, n0, term)

    def by_rows(run):
        @pl.when(jnp.logical_not(last))
        def _():
            run(HALF_ROWS)

        @pl.when(last)
        def _():
            run(2 * HALF_ROWS)

    def slots_rs(f, action):
        action(f, 0)

        @pl.when(last)
        def _():
            action(f, 1)

    def rs1(f, slot):
        return remote(
            part.at[f, slot, pl.ds((1 - c) * 4, 4)], sibrecv.at[f, slot],
            r1s.at[f, slot], r1r.at[f, slot], sibling,
        )

    def rs2(f, slot, d):
        return remote(
            chip.at[f, slot, peer_y(d)], yrecv.at[f, slot, y],
            r2s.at[f, slot, d - 1], r2r.at[f, slot, y], {"tensor": peer_y(d) * 2 + c},
        )

    def rs_cross(f, slot):
        rs1(f, slot).wait_recv()
        for d in (2, 1, 3):
            there = peer_y(d)
            total = part[f, slot, c * 4 + there].astype(F32) + sibrecv[f, slot, there].astype(F32)
            chip[f, slot, there] = total.astype(BF16)
            rs2(f, slot, d).start()

    def rs_total(f, slot):
        total = part[f, slot, own].astype(F32) + sibrecv[f, slot, y].astype(F32)
        for d in (1, 3, 2):
            there = peer_y(d)
            here = yrecv.at[f, slot, there]
            remote(here, here, r2s.at[f, slot, d - 1], r2r.at[f, slot, there], sibling).wait_recv()
            total = total + yrecv[f, slot, there].astype(F32)
        return total

    def rs_end(f, slot):
        rs1(f, slot).wait_send()
        for d in (1, 2, 3):
            rs2(f, slot, d).wait_send()

    def hand(f, slot, device):
        return remote(hsrc.at[f, slot], hrecv.at[f, slot], hs.at[f, slot], hr.at[f, slot], device)

    own_rows = pl.ds(pl.multiple_of(own * ROWS_PAD, ROWS_PAD), ROWS_PAD)

    for arr in (SAVED, GRAD):
        slots_of(arr, ag_wait)
    prepare(SAVED, 0, kept_back)
    by_rows(lambda rows: run_back(0, rows, kept_back, lens_back))
    slots_rs(BACK, lambda f, slot: rs1(f, slot).start())

    slots_of(ACTS, ag_wait)
    prepare(ACTS, 2, kept_fwd)
    slots_rs(BACK, rs_cross)
    by_rows(run_forward)
    slots_rs(FORWARD, lambda f, slot: rs1(f, slot).start())

    for arr in (SAVED_2, GRAD_2):
        slots_of(arr, ag_pass)
    slots_rs(FORWARD, rs_cross)

    @pl.when(first)
    def _():
        drop_row = dropped_positions(kept_fwd, real_rows)
        mine = iota((ROWS_PAD, HALF_ROWS), 1) == own * ROWS_PAD + iota((ROWS_PAD, HALF_ROWS), 0)
        drop_col = jnp.sum(jnp.where(mine, drop_row, 0.0), axis=1, keepdims=True)
        pick(ACTS, drop_col, hsrc.at[FORWARD, 1])
        hand(FORWARD, 1, prev_pipe).start()

    def finish_back(f, slot):
        total = rs_total(f, slot)

        def write(x, g):
            x, g = x.astype(F32), g.astype(F32)
            scale = inverse_root(x)
            unrounded = x * scale
            inner_mean = jnp.mean(total * unrounded, axis=1, keepdims=True)
            hsrc[f, slot] = (g + scale * (total - unrounded * inner_mean)).astype(BF16)

        @pl.when(inner)
        def _():
            write(buf[SAVED, slot, own], buf[GRAD, slot, own])

        @pl.when(first)
        def _():
            write(picked[0, own_rows, :], buf[GRAD, slot, own])

        @pl.when(last)
        def _():
            write(
                buf[SAVED, slot, own],
                gpick[0, pl.ds(pl.multiple_of(slot * HALF_ROWS + own * ROWS_PAD, ROWS_PAD), ROWS_PAD), :],
            )

        if slot == 0:

            @pl.when(jnp.logical_not(first))
            def _():
                hand(f, 0, prev_pipe).start()
        else:
            hand(f, 1, next_pipe).start()

    def finish_forward(f, slot):
        total = rs_total(f, slot)

        @pl.when(jnp.logical_not(first))
        def _():
            chip[f, slot, y] = (buf[ACTS, slot, own].astype(F32) + total).astype(BF16)

        @pl.when(first)
        def _():
            chip[f, slot, y] = (picked[2, own_rows, :].astype(F32) + total).astype(BF16)

        if slot == 0:
            hsrc[f, 0] = chip[f, 0, y]

            @pl.when(jnp.logical_not(last))
            def _():
                hand(f, 0, next_pipe).start()

    slots_rs(BACK, finish_back)
    slots_rs(FORWARD, finish_forward)

    for arr in (SAVED_2, GRAD_2):
        slots_of(arr, ag_wait)
    kept_copy.wait_recv()
    lens_copy.wait_recv()
    kept_two = kept2[1:2, :].astype(F32)
    lens_two = lens2[1:2, :].astype(F32)
    prepare(SAVED_2, 1, kept_two)
    by_rows(lambda rows: run_back(1, rows, kept_two, lens_two))

    columns = pl.ds(pl.multiple_of(r * half_width, half_width), half_width)

    def weights(rows):
        def stashed(which, i):
            return stash[which, i, 0:rows, :]

        def ups(which):
            if rows > HALF_ROWS:
                return gpick[which, :, columns]
            return buf[GRAD + 3 * which, 0, :, :, columns].reshape(HALF_ROWS, half_width)

        x0, x1 = normed[0, 0:rows, columns], normed[1, 0:rows, columns]
        gq_out[0] = (tn(x0, stashed(0, 0)) + tn(x1, stashed(1, 0))).astype(BF16)
        gkv_out[...] = (tn(x0, stashed(0, 1)) + tn(x1, stashed(1, 1))).astype(BF16)
        go_out[0] = (tn(stashed(0, 2), ups(0)) + tn(stashed(1, 2), ups(1))).astype(BF16)

    by_rows(weights)

    nothing = jnp.zeros((real_rows, width), BF16)

    def arrived(f, slot):
        hand(f, slot, next_pipe).wait_recv()
        return hrecv[f, slot, 0:real_rows, :]

    for f, out, none, both in ((FORWARD, handed, first, last), (BACK, back, last, first)):

        @pl.when(none)
        def _(out=out):
            out[0, 0, 0] = nothing

        @pl.when(jnp.logical_not(none))
        def _(f=f, out=out):
            out[0, 0, 0] = arrived(f, 0)

        @pl.when(jnp.logical_not(both))
        def _(out=out):
            out[0, 0, 1] = nothing

        @pl.when(both)
        def _(f=f, out=out):
            out[0, 0, 1] = arrived(f, 1)

    for arr in range(5):
        slots_of(arr, ag_end)
    for arr in (SAVED, GRAD):
        slots_of(arr, lambda arr, slot: dp_copy(arr, slot).wait_send())
    kept_copy.wait_send()
    lens_copy.wait_send()
    for f in (BACK, FORWARD):
        slots_rs(f, rs_end)

    @pl.when(jnp.logical_not(last))
    def _():
        hand(FORWARD, 0, next_pipe).wait_send()

    @pl.when(jnp.logical_not(first))
    def _():
        hand(BACK, 0, next_pipe).wait_send()

    @pl.when(first)
    def _():
        hand(FORWARD, 1, next_pipe).wait_send()

    @pl.when(last)
    def _():
        hand(BACK, 1, next_pipe).wait_send()


def local(acts_in, saved_in, out_grad, w_query, w_keyval, w_out, kept_rows, doc_lengths):
    width = acts_in.shape[4]
    cols = w_query.shape[2]
    slab = (ROWS_PAD, width)
    dma = pltpu.SemaphoreType.DMA
    vmem = pl.BlockSpec(memory_space=pltpu.VMEM)
    anywhere = pl.BlockSpec(memory_space=pl.ANY)
    handed, back, gq, gkv, go = pl.pallas_call(
        kernel,
        out_shape=(
            jax.ShapeDtypeStruct(acts_in.shape, BF16),
            jax.ShapeDtypeStruct(acts_in.shape, BF16),
            jax.ShapeDtypeStruct((1, width // 2, cols), BF16),
            jax.ShapeDtypeStruct((width // 2, 2 * HEAD), BF16),
            jax.ShapeDtypeStruct((1, cols, width // 2), BF16),
        ),
        in_specs=[vmem] * 5 + [anywhere] * 3,
        out_specs=[vmem] * 5,
        scratch_shapes=[
            pltpu.VMEM((5, 2, SLABS) + slab, BF16),
            pltpu.VMEM((width, cols), BF16),
            pltpu.VMEM((width, 2 * HEAD), BF16),
            pltpu.VMEM((cols, width), BF16),
            pltpu.VMEM(kept_rows.shape[2:], jnp.int32),
            pltpu.VMEM(doc_lengths.shape[2:], jnp.int32),
            pltpu.VMEM((3, 2 * HALF_ROWS, width), BF16),
            pltpu.VMEM((3, HALF_ROWS, width), BF16),
            pltpu.VMEM((2, 2 * HALF_ROWS, width), BF16),
            pltpu.VMEM((2, 3, 2 * HALF_ROWS, 2 * HEAD), BF16),
            pltpu.VMEM((2, 2, SLABS) + slab, BF16),
            pltpu.VMEM((2, 2, 4) + slab, BF16),
            pltpu.VMEM((2, 2, 4) + slab, BF16),
            pltpu.VMEM((2, 2, 4) + slab, BF16),
            pltpu.VMEM((2, 2) + slab, BF16),
            pltpu.VMEM((2, 2) + slab, BF16),
            dma((3,)),
            dma((3, 2)),
            dma((3, 2)),
            dma((5, 2, 7)),
            dma((5, 2, SLABS)),
            dma((2, 2)),
            dma((2, 2)),
            dma((2, 2, 3)),
            dma((2, 2, 4)),
            dma((2, 2)),
            dma((2, 2)),
        ],
        compiler_params=pltpu.CompilerParams(
            collective_id=0, has_side_effects=True, vmem_limit_bytes=56 * 1024 * 1024
        ),
        cost_estimate=pl.CostEstimate(flops=4_000_000_000, bytes_accessed=8_000_000, transcendentals=200_000),
        name="section",
    )(
        acts_in, saved_in, out_grad, kept_rows, doc_lengths, w_query,
        w_keyval.reshape(width, 2 * HEAD), w_out,
    )
    return (handed, back, gq, gkv.reshape(1, width // 2, 2, HEAD), go)


def solution(mesh):
    placed = (
        P("pipe", "dp", None, "tensor", None),
        P("pipe", "dp", None, "tensor", None),
        P("pipe", "dp", None, "tensor", None),
        P("pipe", None, "tensor"),
        P("pipe", None, None, "tensor"),
        P("pipe", "tensor", None),
        P("pipe", "dp", None, None),
        P("pipe", "dp", None, None),
    )
    return jax.shard_map(
        local,
        mesh=mesh,
        in_specs=placed,
        out_specs=(
            P("pipe", "dp", None, "tensor", None),
            P("pipe", "dp", None, "tensor", None),
            P("pipe", "dp", "tensor"),
            P("pipe", "dp", None, "tensor"),
            P("pipe", "tensor", "dp"),
        ),
        check_vma=False,
    )
```

time: 473 us -> 77.4 us (0.16)
  waiting for transfers between devices: 315 us -> 0 us
  Pallas kernels: 0 us -> 64.4 us
  blocking collectives: 47.3 us -> 0 us
  other arithmetic: 29.5 us -> 0 us
  local copies, waits for them, and re-layouts: 36.9 us -> 12 us
  starting transfers between devices: 18.6 us -> 0 us
  between operations: 15.1 us -> 0.66 us
  matrix products: 8.86 us -> 0 us
    reduce_scatter x2 -> x0, waiting for transfers between devices: 136 us -> none  [the longest x1 69 us: local(): lax.psum_scatter(grad_o_local.astype(jnp.bfloat16), 'dp', scatter_dimensi...]
    unnamed x5 -> x0, waiting for transfers between devices: 115 us -> none
    pallas_call x0 -> x1, Pallas kernels: none -> 64.4 us  [local(): pl.pallas_call(kernel, out_shape=(jax.ShapeDtypeStruct(acts_in.shape, BF1...]
    psum x1 -> x0, waiting for transfers between devices: 54.3 us -> none  [tensor_total(): return lax.psum(terms.astype(jnp.bfloat16), 'tensor').astype(jnp.float32)]
    all_gather x3 -> x0, blocking collectives: 47.3 us -> none  [the longest x1 20.4 us: local(): lax.all_gather(saved_in, 'tensor', axis=3, tiled=True)]
    ppermute x4 -> x0, starting transfers between devices: 18.5 us -> none  [from_behind(): return lax.ppermute(block, axis, route)]
    gather x10 -> x0, local copies, waits for them, and re-layouts: 14.4 us -> none  [the longest x1 2.02 us: local(): jnp.take(straight, inverse_fwd, axis=0)]
    sort x4 -> x0, other arithmetic: 12.7 us -> none  [the longest x2 6.34 us: arrange(): inverse = jnp.argsort(row_order, stable=True)]
  transfers between devices with their start and end apart: 8 -> 0, of which waited for: 6 -> 0; matrix products, arithmetic and copies ran while one was open for 5% -> 0% of each run, Pallas kernels for 0% -> 0%
where the time goes in v1:
time: 77.4 us; the launch traced here: 77.1 us
  Pallas kernels  64.4 us (83%)
  local copies, waits for them, and re-layouts  12 us (16%)
    pallas_call x1, Pallas kernels, local(): pl.pallas_call(kernel, out_shape=(jax.ShapeDtypeStruct(acts_in.shape, BF1...  64.4 us
    unnamed x18, local copies, waits for them, and re-layouts  9.99 us
    reshape x1, local copies, waits for them, and re-layouts, local(): return (handed, back, gq, gkv.reshape(1, width // 2, 2, HEAD), go)  2.02 us

profile of v1, /device:TPU:1, one launch (start us, length us, event | category | flops | bytes accessed | tf_op | source)
XLA Modules:
  0.0 77.1 jit_solution(10556452706553911790)
XLA Ops:
  0.6 0.0 copy-start.3
  0.6 1.6 %copy.13.acts = bf16[1,1,2,12,2048]{4,3,2,1,0:T(8,128)(2,1)} copy(bf16[1,1,2,12,2048]{4,2,3,1,0:T(2,128)(2,1)} %param.8) | data formatting | bytes 196608 | tf_op args[0]
  2.3 0.0 copy-done.3
  2.3 0.0 copy-start.4
  2.3 0.7 copy.14.saved
  2.9 0.2 copy-done.4
  3.2 0.7 copy.15.ograd
  3.8 2.3 %copy.20 = bf16[256,8,2,128]{3,1,2,0:T(8,128)(2,1)} copy(bf16[256,8,2,128]{3,2,1,0:T(2,128)(2,1)} %bitcast.5) | data formatting | bytes 2097152
  6.2 64.4 %section.1 = (bf16[1,1,2,12,2048]{4,3,2,1,0:T(8,128)(2,1)}, bf16[1,1,2,12,2048]{4,3,2,1,0:T(8,128)(2,1)}, bf16[1,1024,256]{2,1,0:T(8,128)(2,1)}, bf16[1024,256]{1,0:T(8,128)(2,1)}, bf16[1,256,1024]{2,1,0:T(8,128)(2,1)}) custom-call(bf16[1,1,2,12,2048]{4,3,2,1,0:T(8,128)(2,1)} %copy.13.acts, bf16[1,1,2,12,2048]{4,3,2,1,0:T(8,128)(2,1)} %copy.14.saved, ...), custom_call_target="tpu_custom_call" | custom-call | flops 4000000000 | bytes 8000000 | tf_op jit(solution)/shard_map/section/pallas_call | solution.py:545
  70.6 0.0 copy-start.2
  70.6 1.7 %copy.16 = bf16[1,1,2,12,2048]{4,2,3,1,0:T(2,128)(2,1)} copy(bf16[1,1,2,12,2048]{4,3,2,1,0:T(8,128)(2,1)} %get-tuple-element.15) | data formatting | bytes 196608
  72.3 0.0 copy-done.2
  72.3 0.7 copy.17
  73.0 0.0 copy-start.1
  73.0 2.0 %reshape.17 = bf16[1,1024,2,128]{3,2,1,0:T(2,128)(2,1)} reshape(bf16[1024,256]{1,0:T(8,128)(2,1)} %get-tuple-element.13) | data formatting | bytes 1048576 | tf_op jit(solution)/shard_map/reshape | solution.py:594
  75.0 0.0 copy-done.1
  75.0 0.0 copy-start
  75.0 0.8 %copy.23 = bf16[1,1024,256]{2,1,0:T(8,128)(2,1)} copy(bf16[1,1024,256]{2,1,0:T(8,128)(2,1)S(1)} %copy-done.1) | data formatting | bytes 1048576
  75.8 0.4 copy-done
  76.3 0.8 %copy.24 = bf16[1,256,1024]{2,1,0:T(8,128)(2,1)} copy(bf16[1,256,1024]{2,1,0:T(8,128)(2,1)S(1)} %copy-done) | data formatting | bytes 1048576
Async XLA Ops:
  0.6 1.6 %copy-start.3 = (bf16[1,1,2,12,2048]{4,2,3,1,0:T(2,128)(2,1)S(1)}, bf16[1,1,2,12,2048]{4,2,3,1,0:T(2,128)(2,1)}, u32[]{:S(2)}) copy-start(bf16[1,1,2,12,2048]{4,2,3,1,0:T(2,128)(2,1)} %param.9) | copy-start | bytes 294916
  2.3 0.9 %copy-start.4 = (bf16[1,1,2,12,2048]{4,2,3,1,0:T(2,128)(2,1)S(1)}, bf16[1,1,2,12,2048]{4,2,3,1,0:T(2,128)(2,1)}, u32[]{:S(2)}) copy-start(bf16[1,1,2,12,2048]{4,2,3,1,0:T(2,128)(2,1)} %param.10) | copy-start | bytes 294916
  70.6 1.7 %copy-start.2 = (bf16[1,1,2,12,2048]{4,3,2,1,0:T(8,128)(2,1)S(1)}, bf16[1,1,2,12,2048]{4,3,2,1,0:T(8,128)(2,1)}, u32[]{:S(2)}) copy-start(bf16[1,1,2,12,2048]{4,3,2,1,0:T(8,128)(2,1)} %get-tuple-element.16) | copy-start | bytes 294916
  73.0 2.0 %copy-start.1 = (bf16[1,1024,256]{2,1,0:T(8,128)(2,1)S(1)}, bf16[1,1024,256]{2,1,0:T(8,128)(2,1)}, u32[]{:S(2)}) copy-start(bf16[1,1024,256]{2,1,0:T(8,128)(2,1)} %get-tuple-element.27) | copy-start | bytes 1572868
  75.0 1.2 %copy-start = (bf16[1,256,1024]{2,1,0:T(8,128)(2,1)S(1)}, bf16[1,256,1024]{2,1,0:T(8,128)(2,1)}, u32[]{:S(2)}) copy-start(bf16[1,256,1024]{2,1,0:T(8,128)(2,1)} %get-tuple-element.29) | copy-start | bytes 1572868

commit v2 on v1

v2 whole, which is shorter than its diff:
```python
import jax
import jax.numpy as jnp
from jax import lax
from jax.experimental import pallas as pl
from jax.experimental.pallas import tpu as pltpu
from jax.sharding import PartitionSpec as P

HEAD = 128
EPSILON = 1e-06
MESH = pl.DeviceIdType.MESH
F32 = jnp.float32
BF16 = jnp.bfloat16

SAVED, GRAD, ACTS, SAVED_2, GRAD_2 = range(5)
BACK, FORWARD = 0, 1
ROWS_PAD = 16
SLABS = 8
HALF_ROWS = SLABS * ROWS_PAD


def nn(a, b):
    return lax.dot_general(a, b, (((1,), (0,)), ((), ())), preferred_element_type=F32)


def nt(a, b):
    return lax.dot_general(a, b, (((1,), (1,)), ((), ())), preferred_element_type=F32)


def tn(a, b):
    return lax.dot_general(a, b, (((0,), (0,)), ((), ())), preferred_element_type=F32)


def iota(shape, dim):
    return lax.broadcasted_iota(jnp.int32, shape, dim)


def list_index(a, real_rows):
    core, y, r = a // 64, (a // 16) % 4, a % 16
    return (2 * y + core) * real_rows + r, r < real_rows


def to_row(col):
    n = col.shape[0]
    return jnp.sum(jnp.where(iota((n, n), 0) == iota((n, n), 1), col, 0.0), axis=0, keepdims=True)


def to_col(row):
    n = row.shape[1]
    return jnp.sum(jnp.where(iota((n, n), 0) == iota((n, n), 1), row, 0.0), axis=1, keepdims=True)


def kept_positions(kept, real_rows):
    keep = kept.shape[1]
    place, real = list_index(iota((HALF_ROWS, keep), 0), real_rows)
    hit = (place == iota((HALF_ROWS, keep), 1)) & real
    found = jnp.sum(jnp.where(hit, kept, 0.0), axis=1, keepdims=True)
    _, real_col = list_index(iota((HALF_ROWS, 1), 0), real_rows)
    return jnp.where(real_col, found, 1000.0)


def dropped_positions(kept, real_rows):
    keep = kept.shape[1]
    n = 256
    named = jnp.max(
        jnp.where(iota((n, keep), 0).astype(F32) == kept, 1.0, 0.0), axis=1, keepdims=True
    )
    free = jnp.where(iota((n, 1), 0) < 2 * keep, 1.0 - named, 0.0)
    count = jnp.sum(
        jnp.where(iota((n, n), 1) <= iota((n, n), 0), to_row(free), 0.0), axis=1, keepdims=True
    )
    place, real = list_index(iota((n, HALF_ROWS), 1), real_rows)
    hit = (count - 1.0 == place.astype(F32)) & (free > 0.5) & real
    found = jnp.sum(jnp.where(hit, iota((n, HALF_ROWS), 0).astype(F32), 0.0), axis=0, keepdims=True)
    _, real_row = list_index(iota((1, HALF_ROWS), 1), real_rows)
    return jnp.where(real_row, found, 1000.0)


def document_of(positions, lengths):
    bound = jnp.zeros((1, 1), F32)
    total = jnp.zeros(positions.shape, F32)
    for m in range(lengths.shape[1]):
        bound = bound + lengths[:, m : m + 1]
        total = total + jnp.where(positions >= bound, 1.0, 0.0)
    return total


def select(pos_col, real_rows, keep):
    n = 2 * HALF_ROWS
    b = iota((1, n), 1)
    place, real = list_index(b % HALF_ROWS, real_rows)
    flat = jnp.where(real, (b // HALF_ROWS) * keep + place, -1).astype(F32)
    return jnp.where(pos_col == flat, 1.0, 0.0).astype(BF16)


def line_of(q, width):
    tile, slot, r = q // (2 * ROWS_PAD), (q // ROWS_PAD) % 2, q % ROWS_PAD
    quarter = width // HEAD // 4
    spill = r >= 12
    row = jnp.where(spill, 4 * (tile // quarter) + r - 12, r)
    place = jnp.where(spill, 3 * quarter + tile % quarter, tile)
    return (row * (4 * quarter) + place) * 2 + slot


def unpack(x):
    w = x.shape[1] // 3
    r = iota((ROWS_PAD, 1), 0)
    tail = jnp.where(
        r < 4,
        pltpu.roll(x[:, :w], 4, 0),
        jnp.where(r < 8, pltpu.roll(x[:, w : 2 * w], 8, 0), pltpu.roll(x[:, 2 * w :], 12, 0)),
    )
    return jnp.where(r < 12, jnp.concatenate([x, tail], axis=1), 0.0)


def pack(parts, tail):
    r = iota((tail.shape[0], 1), 0) % ROWS_PAD
    return [jnp.where(r < 12, x, pltpu.roll(tail, 12 - 4 * i, 0)) for i, x in enumerate(parts)]


def pack_slab(x):
    w = x.shape[1] // 4
    return jnp.concatenate(pack([x[:, i * w : (i + 1) * w] for i in range(3)], x[:, 3 * w :]), axis=1)


def pairs_apart():
    n = 2 * HEAD
    q, k = iota((n, n), 0), iota((n, n), 1)
    return jnp.where((q % HEAD) * 2 + q // HEAD == k, 1.0, 0.0).astype(BF16)


def inverse_root(x):
    return lax.rsqrt(jnp.mean(x * x, axis=1, keepdims=True) + EPSILON)


def kernel(
    acts_hbm, saved_hbm, ograd_hbm, kept_hbm, lens_hbm, wq_hbm, wkv_hbm, wo_hbm,
    handed_out, back_out, gq_out, gkv_out, go_out,
    acts, saved, ograd, kept, lens, buf, wq, wkv, wkv_pairs, wo, kept2, lens2, normed, raw, picked, chosen, stash, part, sibrecv, chip, yrecv, hsrc, hrecv,
    tiles, handed, back, gq, gkv, go,
    wsem, osem, dps, dpr, ags, agr, r1s, r1r, r2s, r2r, hs, hr,
):
    pipes = lax.axis_size("pipe")
    p, r, t = lax.axis_index("pipe"), lax.axis_index("dp"), lax.axis_index("tensor")
    y, c = t // 2, t % 2
    own = c * 4 + y
    first, last = p == 0, p == pipes - 1
    inner = jnp.logical_not(first | last)
    width = wq.shape[0]
    real_rows = acts.shape[0] * HEAD // (2 * width)
    keep = kept.shape[3]
    half_width, packed, quarter = width // 2, 3 * width // 4, width // 4
    next_pipe = {"pipe": lax.rem(p + 1, pipes)}
    prev_pipe = {"pipe": lax.rem(p + pipes - 1, pipes)}
    sibling = {"tensor": y * 2 + 1 - c}
    other_dp = {"dp": 1 - r}

    def peer_y(d):
        return lax.rem(y + d, 4)

    def remote(src, dst, send, recv, device):
        return pltpu.make_async_remote_copy(
            src_ref=src, dst_ref=dst, send_sem=send, recv_sem=recv, device_id=device, device_id_type=MESH
        )

    barrier = pltpu.get_barrier_semaphore()
    greet = [{"tensor": lax.rem(t + d, 8)} for d in range(1, 8)] + [other_dp, next_pipe, prev_pipe]
    for device in greet:
        pl.semaphore_signal(barrier, inc=1, device_id=device, device_id_type=MESH)

    loads = [
        pltpu.make_async_copy(src, dst, wsem.at[i])
        for i, (src, dst) in enumerate(
            (
                (saved_hbm, saved),
                (ograd_hbm, ograd),
                (acts_hbm, acts),
                (kept_hbm, kept),
                (lens_hbm, lens),
                (wkv_hbm, wkv_pairs),
                (wq_hbm.at[0], wq),
                (wo_hbm.at[0], wo),
            )
        )
    ]
    for load in loads:
        load.start()
    stores = [
        pltpu.make_async_copy(src, dst, osem.at[i])
        for i, (src, dst) in enumerate(
            ((handed, handed_out), (back, back_out), (gq, gq_out), (gkv, gkv_out), (go, go_out))
        )
    ]
    tiles[...] = jnp.zeros_like(tiles)

    lines = acts.shape[0]
    q, k = iota((lines, lines), 0), iota((lines, lines), 1)
    spread = jnp.where(line_of(q, width) == k, 1.0, 0.0).astype(BF16)
    for load in loads[:5]:
        load.wait()
    rows = nn(spread, jnp.concatenate([saved[...], ograd[...], acts[...]], axis=1)).astype(BF16)
    for ct in range(packed // HEAD):
        for slot in range(2):
            for arr in (SAVED, GRAD, ACTS):
                at = (2 * ct + slot) * ROWS_PAD
                buf[arr, slot, own, :, ct * HEAD : (ct + 1) * HEAD] = rows[
                    at : at + ROWS_PAD, arr * HEAD : (arr + 1) * HEAD
                ]

    pl.semaphore_wait(barrier, len(greet))

    def dp_copy(arr, slot):
        return remote(
            buf.at[arr, slot, own], buf.at[arr + 3, slot, own],
            dps.at[arr, slot], dpr.at[arr, slot], other_dp,
        )

    kept_copy = remote(kept.at[0, 0], kept2, dps.at[2, 0], dpr.at[2, 0], other_dp)
    lens_copy = remote(lens.at[0, 0], lens2, dps.at[2, 1], dpr.at[2, 1], other_dp)

    def slab_to(arr, slot, slab, sem, device):
        here = buf.at[arr, slot, slab]
        return remote(here, here, ags.at[arr, slot, sem], agr.at[arr, slot, slab], device)

    def across(sem, slab, arr, slot, d):
        slab_to(arr, slot, slab, sem, {"tensor": peer_y(d) * 2 + c}).start()

    def ag_take(arr, slot, d):
        copy = slab_to(arr, slot, c * 4 + peer_y(d), 3 + d, sibling)
        copy.wait_recv()
        copy.start()

    def ag_rest(arr, slot):
        ag_take(arr, slot, 1 if (arr + slot) % 2 == 0 else 3)
        ag_take(arr, slot, 2)

    def ag_wait(arr, slot):
        for d in range(4):
            slab_to(arr, slot, (1 - c) * 4 + peer_y(d), 3, sibling).wait_recv()

    def ag_end(arr, slot):
        for d in range(7):
            slab_to(arr, slot, own, d, sibling).wait_send()

    def split_weights():
        loads[5].wait()
        apart = pairs_apart()

        def split(i, carry):
            two = pl.multiple_of(i * 512, 512)
            pairs = jnp.concatenate(
                [wkv_pairs[pl.ds(two, 256), :], wkv_pairs[pl.ds(two + 256, 256), :]], axis=1
            )
            got = nn(apart, pairs).astype(BF16)
            for j in range(2):
                at = pl.ds(pl.multiple_of(i * 256 + j * 128, 128), 128)
                cols = slice(j * HEAD, (j + 1) * HEAD)
                wkv[at, 0:HEAD] = got[:HEAD, cols]
                wkv[at, HEAD:] = got[HEAD:, cols]
            return carry

        lax.fori_loop(0, width // 256, split, 0)
        for load in loads[6:]:
            load.wait()

    def slab_rows(i):
        return pl.ds(pl.multiple_of(i * ROWS_PAD, ROWS_PAD), ROWS_PAD)

    def for_slabs(slabs, step):
        lax.fori_loop(0, slabs, lambda i, carry: step(i) or carry, 0, unroll=2)

    def received(arr, i):
        return unpack(buf[arr, i // SLABS, i % SLABS].astype(F32))

    def to_raw(arr, slabs):
        def step(i):
            raw[arr, slab_rows(i), :] = received(arr, i).astype(BF16)

        for_slabs(slabs, step)

    def normalise(which, slab_of, slabs):
        def step(i):
            x = slab_of(i)
            normed[which, slab_rows(i), :] = (x * inverse_root(x)).astype(BF16)

        for_slabs(slabs, step)

    def places(kept_list, lengths, rows):
        pos_col = kept_positions(kept_list, real_rows)
        pos_row = to_row(pos_col)
        if rows > HALF_ROWS:
            more = dropped_positions(kept_list, real_rows)
            pos_row = jnp.concatenate([pos_row, more], axis=1)
            pos_col = jnp.concatenate([pos_col, to_col(more)], axis=0)
        allowed = (document_of(pos_col, lengths) == document_of(pos_row, lengths)) & (
            pos_row <= pos_col
        )
        return pos_col, allowed

    def heads(which, rows, allowed):
        x = normed[which, 0:rows, :]
        queries = nn(x, wq[...]).astype(BF16)
        keyval = nn(x, wkv[...]).astype(BF16)
        keys, values = keyval[:, :HEAD], keyval[:, HEAD:]
        out = []
        for h in range(2):
            q = queries[:, h * HEAD : (h + 1) * HEAD]
            scores = jnp.where(allowed, nt(q, keys) * HEAD ** (-0.5), -jnp.inf)
            e = jnp.exp(scores - jnp.max(scores, axis=1, keepdims=True))
            probs = e / jnp.sum(e, axis=1, keepdims=True)
            rounded = probs.astype(BF16)
            out.append((q, probs, rounded, nn(rounded, values).astype(BF16)))
        return keys, values, out

    def store_part(f, rows, term):
        packs = pack([term(i * quarter) for i in range(3)], term(3 * quarter))
        for i, value in enumerate(packs):
            value = value.astype(BF16)
            for slot in range(rows // HALF_ROWS):
                part[f, slot, :, :, i * quarter : (i + 1) * quarter] = value[
                    slot * HALF_ROWS : (slot + 1) * HALF_ROWS
                ].reshape(SLABS, ROWS_PAD, quarter)

    def run_forward(rows, allowed):
        _, _, out = heads(2, rows, allowed)
        mixed = jnp.concatenate([o[3] for o in out], axis=1)
        store_part(FORWARD, rows, lambda n0: nn(mixed, wo[:, n0 : n0 + quarter]))

    def run_back(which, rows, pos_col, allowed, middle, late):
        keys, values, out = heads(which, rows, allowed)
        middle()
        to_raw(GRAD + 3 * which, rows // ROWS_PAD)
        upstream = raw[GRAD + 3 * which, 0:rows, :]
        grad_mixed = nt(upstream, wo[...]).astype(BF16)
        mixed = jnp.concatenate([o[3] for o in out], axis=1)
        if rows > HALF_ROWS:
            picks = select(pos_col, real_rows, keep)
            grad_mixed = nn(picks, grad_mixed).astype(BF16)
            mixed = tn(picks, mixed).astype(BF16)
            if which == 0:
                chosen[...] = picks
        grad_k = jnp.zeros((rows, HEAD), F32)
        grad_v = jnp.zeros((rows, HEAD), F32)
        grad_q = []
        for h, (q, probs, rounded, _) in enumerate(out):
            gm = grad_mixed[:, h * HEAD : (h + 1) * HEAD]
            grad_probs = nt(gm, values)
            centre = jnp.sum(probs * grad_probs, axis=1, keepdims=True)
            scores = (probs * (grad_probs - centre) * HEAD ** (-0.5)).astype(BF16)
            grad_q.append(nn(scores, keys).astype(BF16))
            grad_k = grad_k + tn(scores, q)
            grad_v = grad_v + tn(rounded, gm)
        gq_rows = jnp.concatenate(grad_q, axis=1)
        gkv_rows = jnp.concatenate([grad_k.astype(BF16), grad_v.astype(BF16)], axis=1)
        stash[which, 0, 0:rows, :] = gq_rows
        stash[which, 1, 0:rows, :] = gkv_rows
        stash[which, 2, 0:rows, :] = mixed
        late()
        if which == 0:
            store_part(
                BACK,
                rows,
                lambda n0: nt(gq_rows, wq[n0 : n0 + quarter, :]) + nt(gkv_rows, wkv[n0 : n0 + quarter, :]),
            )

    def rs1(f, slot):
        return remote(
            part.at[f, slot, pl.ds((1 - c) * 4, 4)], sibrecv.at[f, slot],
            r1s.at[f, slot], r1r.at[f, slot], sibling,
        )

    def rs_send(f, slot):
        rs1(f, slot).start()

    def rs2(f, slot, d):
        return remote(
            chip.at[f, slot, peer_y(d)], yrecv.at[f, slot, y],
            r2s.at[f, slot, d - 1], r2r.at[f, slot, y], {"tensor": peer_y(d) * 2 + c},
        )

    def rs_cross(f, slot):
        rs1(f, slot).wait_recv()
        for d in (2, 1, 3):
            there = peer_y(d)
            total = part[f, slot, c * 4 + there].astype(F32) + sibrecv[f, slot, there].astype(F32)
            chip[f, slot, there] = total.astype(BF16)
            rs2(f, slot, d).start()

    def rs_total(f, slot):
        total = part[f, slot, own].astype(F32) + sibrecv[f, slot, y].astype(F32)
        for d in (1, 3, 2):
            there = peer_y(d)
            here = yrecv.at[f, slot, there]
            remote(here, here, r2s.at[f, slot, d - 1], r2r.at[f, slot, there], sibling).wait_recv()
            total = total + yrecv[f, slot, there].astype(F32)
        return unpack(total)

    def rs_end(f, slot):
        rs1(f, slot).wait_send()
        for d in (1, 2, 3):
            rs2(f, slot, d).wait_send()

    def hand(f, slot, device):
        return remote(hsrc.at[f, slot], hrecv.at[f, slot], hs.at[f, slot], hr.at[f, slot], device)

    columns = pl.ds(pl.multiple_of(r * half_width, half_width), half_width)

    def weights(rows):
        def stashed(which, i):
            return stash[which, i, 0:rows, :]

        def ups(which):
            return raw[GRAD + 3 * which, 0:rows, columns]

        x0, x1 = normed[0, 0:rows, columns], normed[1, 0:rows, columns]
        go[...] = (tn(stashed(0, 2), ups(0)) + tn(stashed(1, 2), ups(1))).astype(BF16)
        stores[4].start()
        gq[...] = (tn(x0, stashed(0, 0)) + tn(x1, stashed(1, 0))).astype(BF16)
        stores[2].start()
        both = (tn(x0, stashed(0, 1)) + tn(x1, stashed(1, 1))).astype(BF16)
        joined = jnp.transpose(pairs_apart().astype(F32)).astype(BF16)
        for i in range(half_width // HEAD):
            block = both[i * HEAD : (i + 1) * HEAD]
            block = jnp.concatenate([block[:, :HEAD], block[:, HEAD:]], axis=0)
            gkv[i * 256 : (i + 1) * 256, :] = nn(joined, block).astype(BF16)
        stores[3].start()

    def section(at_first, at_last):
        rows = 2 * HALF_ROWS if at_last else HALF_ROWS
        ends = at_first or at_last

        def slots_of(arr, action):
            two = at_last or (at_first and arr not in (GRAD, GRAD_2))
            for slot in range(2 if two else 1):
                action(arr, slot)

        def slots_rs(f, action):
            for slot in (1, 0) if at_last else (0,):
                action(f, slot)

        def ag_start(arr, slot):
            if not ends:
                across(1, own, arr, slot, 2)
            across(0, own, arr, slot, 1)
            across(2, own, arr, slot, 3)
            slab_to(arr, slot, own, 3, sibling).start()

        def ag_near(arr, slot):
            source, target = (3, 1) if (arr + slot) % 2 == 0 else (1, 3)
            ag_take(arr, slot, source)
            if ends:
                across(1, c * 4 + peer_y(source), arr, slot, target)

        def near(*arrs):
            for arr in arrs:
                slots_of(arr, ag_near)

        def rest(*arrs):
            for arr in arrs:
                slots_of(arr, ag_rest)

        def relay():
            def one(arr, slot):
                dp_copy(arr, slot).wait_recv()
                ag_start(arr + 3, slot)

            slots_of(SAVED, one)
            slots_of(GRAD, one)

        def prepare(arr, which, pos_col):
            slots_of(arr, ag_wait)
            if at_first:
                to_raw(arr, 2 * SLABS)
                picks = select(pos_col, real_rows, keep)
                for n0 in range(0, width, quarter):
                    picked[which, :, n0 : n0 + quarter] = nn(
                        picks, raw[arr, :, n0 : n0 + quarter]
                    ).astype(BF16)
                normalise(which, lambda i: picked[which, slab_rows(i), :].astype(F32), SLABS)
            else:
                normalise(which, lambda i: received(arr, i), rows // ROWS_PAD)

        def finish_back(f, slot):
            total = rs_total(f, slot)
            at = slot * SLABS + own
            x = picked[0, slab_rows(own), :].astype(F32) if at_first else received(SAVED, at)
            if at_last:
                g = nn(chosen[slab_rows(at), :], raw[GRAD])
            else:
                g = raw[GRAD, slab_rows(own), :].astype(F32)
            scale = inverse_root(x)
            unrounded = x * scale
            inner_mean = jnp.mean(total * unrounded, axis=1, keepdims=True)
            hsrc[f, slot] = pack_slab(g + scale * (total - unrounded * inner_mean)).astype(BF16)
            if slot == 1:
                hand(f, 1, next_pipe).start()
            elif not at_first:
                hand(f, 0, prev_pipe).start()

        def finish_forward(f, slot):
            total = rs_total(f, slot)
            x = picked[2, slab_rows(own), :].astype(F32) if at_first else received(ACTS, slot * SLABS + own)
            hsrc[f, slot] = pack_slab(x + total).astype(BF16)
            if not at_last:
                hand(f, 0, next_pipe).start()

        def nothing():
            pass

        slots_of(SAVED, lambda arr, slot: dp_copy(arr, slot).start())
        slots_of(GRAD, lambda arr, slot: dp_copy(arr, slot).start())
        kept_copy.start()
        lens_copy.start()
        for arr in (SAVED, GRAD) if at_last else (ACTS, SAVED, GRAD):
            slots_of(arr, ag_start)
        split_weights()
        pos_fwd, allowed_fwd = places(kept[0, 0, 0:1, :].astype(F32), lens[0, 0, 0:1, :].astype(F32), rows)
        pos_back, allowed_back = places(kept[0, 0, 1:2, :].astype(F32), lens[0, 0, 1:2, :].astype(F32), rows)

        if at_last:
            near(SAVED, GRAD)
            slots_of(ACTS, ag_start)
            rest(SAVED, GRAD)
            prepare(SAVED, 0, pos_back)

            def middle():
                near(ACTS)
                slots_of(GRAD, ag_wait)

            run_back(0, rows, pos_back, allowed_back, middle, lambda: rest(ACTS))
            slots_rs(BACK, rs_send)
            slots_rs(BACK, rs_cross)
            relay()
            prepare(ACTS, 2, pos_fwd)
            slots_rs(BACK, finish_back)
            near(SAVED_2, GRAD_2)
            run_forward(rows, allowed_fwd)
            slots_rs(FORWARD, rs_send)
            rest(SAVED_2, GRAD_2)
            slots_rs(FORWARD, rs_cross)
        else:
            near(ACTS)
            if at_first:
                near(SAVED, GRAD)
            rest(ACTS)
            prepare(ACTS, 2, pos_fwd)
            if at_first:
                drop_row = dropped_positions(kept[0, 0, 0:1, :].astype(F32), real_rows)
                mine = iota((ROWS_PAD, HALF_ROWS), 1) == own * ROWS_PAD + iota((ROWS_PAD, HALF_ROWS), 0)
                drop_col = jnp.sum(jnp.where(mine, drop_row, 0.0), axis=1, keepdims=True)
                hsrc[FORWARD, 1] = pack_slab(nn(select(drop_col, real_rows, keep), raw[ACTS])).astype(BF16)
                hand(FORWARD, 1, prev_pipe).start()
            run_forward(rows, allowed_fwd)
            slots_rs(FORWARD, rs_send)
            if not at_first:
                near(SAVED, GRAD)
            rest(SAVED, GRAD)
            slots_rs(FORWARD, rs_cross)
            prepare(SAVED, 0, pos_back)
            run_back(0, rows, pos_back, allowed_back, lambda: slots_of(GRAD, ag_wait), nothing)
            slots_rs(BACK, rs_send)
            slots_rs(FORWARD, finish_forward)
            slots_rs(BACK, rs_cross)
            relay()
            slots_rs(BACK, finish_back)
            near(SAVED_2, GRAD_2)
            rest(SAVED_2, GRAD_2)

        kept_copy.wait_recv()
        lens_copy.wait_recv()
        pos_two, allowed_two = places(kept2[1:2, :].astype(F32), lens2[1:2, :].astype(F32), rows)
        prepare(SAVED_2, 1, pos_two)
        run_back(1, rows, pos_two, allowed_two, lambda: slots_of(GRAD_2, ag_wait), nothing)
        if at_last:
            slots_rs(FORWARD, finish_forward)
        weights(rows)

        for f, none, two in ((FORWARD, at_first, at_last), (BACK, at_last, at_first)):
            for slot in ([] if none else [0]) + ([1] if two else []):
                hand(f, slot, next_pipe).wait_recv()
                for ct in range(packed // HEAD):
                    at = (2 * ct + slot) * ROWS_PAD
                    tiles[at : at + ROWS_PAD, f * HEAD : (f + 1) * HEAD] = hrecv[
                        f, slot, :, ct * HEAD : (ct + 1) * HEAD
                    ]
        q, k = iota((lines, lines), 1), iota((lines, lines), 0)
        gather = jnp.where(line_of(q, width) == k, 1.0, 0.0).astype(BF16)
        found = nn(gather, tiles[...]).astype(BF16)
        handed[...] = found[:, FORWARD * HEAD : (FORWARD + 1) * HEAD]
        back[...] = found[:, BACK * HEAD : (BACK + 1) * HEAD]
        stores[0].start()
        stores[1].start()

        for arr in range(5):
            slots_of(arr, ag_end)
        for arr in (SAVED, GRAD):
            slots_of(arr, lambda arr, slot: dp_copy(arr, slot).wait_send())
        kept_copy.wait_send()
        lens_copy.wait_send()
        for f in (BACK, FORWARD):
            slots_rs(f, rs_end)
        if not at_last:
            hand(FORWARD, 0, next_pipe).wait_send()
        if not at_first:
            hand(BACK, 0, next_pipe).wait_send()
        if at_first:
            hand(FORWARD, 1, next_pipe).wait_send()
        if at_last:
            hand(BACK, 1, next_pipe).wait_send()
        for store in stores:
            store.wait()

    pl.when(inner)(lambda: section(False, False))
    pl.when(first)(lambda: section(True, False))
    pl.when(last)(lambda: section(False, True))


def copy_kernel(*refs):
    ins, outs, held, load, store = refs[:5], refs[5:10], refs[10:15], refs[15], refs[16]
    loads = [pltpu.make_async_copy(ins[i], held[i], load.at[i]) for i in range(5)]
    stores = [pltpu.make_async_copy(held[i], outs[i], store.at[i]) for i in range(5)]
    for copy in loads:
        copy.start()
    for i in range(5):
        loads[i].wait()
        stores[i].start()
    for copy in stores:
        copy.wait()


def lines_of(x):
    _, _, slots, rows, width = x.shape
    x = x.reshape(slots, rows, width // HEAD, HEAD)
    return jnp.transpose(x, (1, 2, 0, 3)).reshape(-1, HEAD)


def from_lines(x, shape):
    _, _, slots, rows, width = shape
    x = x.reshape(rows, width // HEAD, slots, HEAD)
    return jnp.transpose(x, (2, 0, 1, 3)).reshape(shape)


def local(acts_in, saved_in, out_grad, w_query, w_keyval, w_out, kept_rows, doc_lengths):
    width = acts_in.shape[4]
    cols = w_query.shape[2]
    slab = (ROWS_PAD, 3 * width // 4)
    lines = 2 * acts_in.shape[3] * width // HEAD
    dma = pltpu.SemaphoreType.DMA
    anywhere = pl.BlockSpec(memory_space=pl.ANY)
    outs = ((lines, HEAD), (lines, HEAD), (width // 2, cols), (width, HEAD), (cols, width // 2))
    out_shape = tuple(jax.ShapeDtypeStruct(shape, BF16) for shape in outs)
    results = pl.pallas_call(
        kernel,
        out_shape=out_shape,
        in_specs=[anywhere] * 8,
        out_specs=[anywhere] * 5,
        scratch_shapes=[pltpu.VMEM((lines, HEAD), BF16)] * 3
        + [
            pltpu.VMEM(kept_rows.shape, jnp.int32),
            pltpu.VMEM(doc_lengths.shape, jnp.int32),
            pltpu.VMEM((5, 2, SLABS) + slab, BF16),
            pltpu.VMEM((width, cols), BF16),
            pltpu.VMEM((width, 2 * HEAD), BF16),
            pltpu.VMEM((2 * width, HEAD), BF16),
            pltpu.VMEM((cols, width), BF16),
            pltpu.VMEM(kept_rows.shape[2:], jnp.int32),
            pltpu.VMEM(doc_lengths.shape[2:], jnp.int32),
            pltpu.VMEM((3, 2 * HALF_ROWS, width), BF16),
            pltpu.VMEM((5, 2 * HALF_ROWS, width), BF16),
            pltpu.VMEM((3, HALF_ROWS, width), BF16),
            pltpu.VMEM((2 * HALF_ROWS, 2 * HALF_ROWS), BF16),
            pltpu.VMEM((2, 3, 2 * HALF_ROWS, 2 * HEAD), BF16),
            pltpu.VMEM((2, 2, SLABS) + slab, BF16),
            pltpu.VMEM((2, 2, 4) + slab, BF16),
            pltpu.VMEM((2, 2, 4) + slab, BF16),
            pltpu.VMEM((2, 2, 4) + slab, BF16),
            pltpu.VMEM((2, 2) + slab, BF16),
            pltpu.VMEM((2, 2) + slab, BF16),
            pltpu.VMEM((lines, 2 * HEAD), BF16),
        ]
        + [pltpu.VMEM(shape, BF16) for shape in outs]
        + [
            dma((8,)),
            dma((5,)),
            dma((3, 2)),
            dma((3, 2)),
            dma((5, 2, 7)),
            dma((5, 2, SLABS)),
            dma((2, 2)),
            dma((2, 2)),
            dma((2, 2, 3)),
            dma((2, 2, 4)),
            dma((2, 2)),
            dma((2, 2)),
        ],
        compiler_params=pltpu.CompilerParams(
            collective_id=0, has_side_effects=True, vmem_limit_bytes=56 * 1024 * 1024
        ),
        cost_estimate=pl.CostEstimate(flops=4_000_000_000, bytes_accessed=8_000_000, transcendentals=200_000),
        name="section",
    )(
        lines_of(acts_in), lines_of(saved_in), lines_of(out_grad), kept_rows, doc_lengths, w_query,
        w_keyval.reshape(2 * width, HEAD), w_out,
    )
    handed, back, gq, gkv, go = pl.pallas_call(
        copy_kernel,
        out_shape=out_shape,
        in_specs=[anywhere] * 5,
        out_specs=[anywhere] * 5,
        scratch_shapes=[pltpu.VMEM(shape, BF16) for shape in outs] + [dma((5,)), dma((5,))],
        cost_estimate=pl.CostEstimate(flops=0, bytes_accessed=4_000_000, transcendentals=0),
        name="results",
    )(*results)
    return (
        from_lines(handed, acts_in.shape),
        from_lines(back, acts_in.shape),
        gq[None],
        gkv.reshape(1, width // 2, 2, HEAD),
        go[None],
    )


def solution(mesh):
    placed = (
        P("pipe", "dp", None, "tensor", None),
        P("pipe", "dp", None, "tensor", None),
        P("pipe", "dp", None, "tensor", None),
        P("pipe", None, "tensor"),
        P("pipe", None, None, "tensor"),
        P("pipe", "tensor", None),
        P("pipe", "dp", None, None),
        P("pipe", "dp", None, None),
    )
    return jax.shard_map(
        local,
        mesh=mesh,
        in_specs=placed,
        out_specs=(
            P("pipe", "dp", None, "tensor", None),
            P("pipe", "dp", None, "tensor", None),
            P("pipe", "dp", "tensor"),
            P("pipe", "dp", None, "tensor"),
            P("pipe", "tensor", "dp"),
        ),
        check_vma=False,
    )
```

time: 77.4 us -> 58.8 us (0.76)
  local copies, waits for them, and re-layouts: 12 us -> 0 us
  Pallas kernels: 64.4 us -> 57.8 us
    unnamed x18 -> x0, local copies, waits for them, and re-layouts: 9.99 us -> none
    pallas_call x1 -> x2, Pallas kernels: 64.4 us -> 57.8 us  [the longest x1 55.4 us: local(): pl.pallas_call(kernel, out_shape=out_shape, in_specs=[anywhere] * 8, out_...]
    reshape x1 -> x0, local copies, waits for them, and re-layouts: 2.02 us -> none  [local(): return (handed, back, gq, gkv.reshape(1, width // 2, 2, HEAD), go)]
where the time goes in v2:
time: 58.8 us; the launch traced here: 58.6 us
  Pallas kernels  57.8 us (98%)
  between operations  0.82 us (1%)
    pallas_call x1, Pallas kernels, local(): pl.pallas_call(kernel, out_shape=out_shape, in_specs=[anywhere] * 8, out_...  55.4 us
    pallas_call x1, Pallas kernels, local(): pl.pallas_call(copy_kernel, out_shape=out_shape, in_specs=[anywhere] * 5,...  2.37 us

profile of v2, /device:TPU:1, one launch (start us, length us, event | category | flops | bytes accessed | tf_op | source)
XLA Modules:
  0.0 58.6 jit_solution(13346542933920904950)
XLA Ops:
  0.6 55.4 %section.1 = (bf16[384,128]{1,0:T(8,128)(2,1)}, bf16[384,128]{1,0:T(8,128)(2,1)}, bf16[1024,256]{1,0:T(8,128)(2,1)}, bf16[2048,128]{1,0:T(8,128)(2,1)}, bf16[256,1024]{1,0:T(8,128)(2,1)}) custom-call(bf16[384,128]{1,0:T(8,128)(2,1)} %bitcast.33, bf16[384,128]{1,0:T(8,128)(2,1)} %bitcast.34, bf16[384,128]{1,0:T(8,128)(2,1)} %bitcast.35, ...), custom_call_target="tpu_custom_call" | custom-call | flops 4000000000 | bytes 8000000 | tf_op jit(solution)/shard_map/section/pallas_call | solution.py:651
  56.1 2.4 %results.1 = (bf16[384,128]{1,0:T(8,128)(2,1)}, bf16[384,128]{1,0:T(8,128)(2,1)}, bf16[1024,256]{1,0:T(8,128)(2,1)}, bf16[2048,128]{1,0:T(8,128)(2,1)}, bf16[256,1024]{1,0:T(8,128)(2,1)}) custom-call(bf16[384,128]{1,0:T(8,128)(2,1)} %get-tuple-element.15.refs_0_, bf16[384,128]{1,0:T(8,128)(2,1)} %get-tuple-element.16.refs_1_, ...), custom_call_target="tpu_custom_call" | custom-call | bytes 4000000 | tf_op jit(solution)/shard_map/results/pallas_call | solution.py:704

commit v3 on v2

--- a/solution.py
+++ b/solution.py
@@ -437,8 +437,11 @@
             for slot in (1, 0) if at_last else (0,):
                 action(f, slot)
 
+        def direct(arr):
+            return not ends or (at_first and arr in (SAVED_2, GRAD_2))
+
         def ag_start(arr, slot):
-            if not ends:
+            if direct(arr):
                 across(1, own, arr, slot, 2)
             across(0, own, arr, slot, 1)
             across(2, own, arr, slot, 3)
@@ -447,7 +450,7 @@
         def ag_near(arr, slot):
             source, target = (3, 1) if (arr + slot) % 2 == 0 else (1, 3)
             ag_take(arr, slot, source)
-            if ends:
+            if not direct(arr):
                 across(1, c * 4 + peer_y(source), arr, slot, target)
 
         def near(*arrs):
@@ -556,14 +559,19 @@
             rest(SAVED, GRAD)
             slots_rs(FORWARD, rs_cross)
             prepare(SAVED, 0, pos_back)
+            if at_first:
+                relay()
             run_back(0, rows, pos_back, allowed_back, lambda: slots_of(GRAD, ag_wait), nothing)
             slots_rs(BACK, rs_send)
             slots_rs(FORWARD, finish_forward)
-            slots_rs(BACK, rs_cross)
-            relay()
-            slots_rs(BACK, finish_back)
+            if not at_first:
+                slots_rs(BACK, rs_cross)
+                relay()
+                slots_rs(BACK, finish_back)
             near(SAVED_2, GRAD_2)
             rest(SAVED_2, GRAD_2)
+            if at_first:
+                slots_rs(BACK, rs_cross)
 
         kept_copy.wait_recv()
         lens_copy.wait_recv()
@@ -572,6 +580,8 @@
         run_back(1, rows, pos_two, allowed_two, lambda: slots_of(GRAD_2, ag_wait), nothing)
         if at_last:
             slots_rs(FORWARD, finish_forward)
+        if at_first:
+            slots_rs(BACK, finish_back)
         weights(rows)
 
         for f, none, two in ((FORWARD, at_first, at_last), (BACK, at_last, at_first)):

time: 58.8 us -> 54.2 us (0.922)
  Pallas kernels: 57.8 us -> 53.3 us
    pallas_call x1, Pallas kernels: 55.4 us -> 50.9 us  [local(): pl.pallas_call(kernel, out_shape=out_shape, in_specs=[anywhere] * 8, out_...]
where the time goes in v3:
time: 54.2 us; the launch traced here: 54.1 us
  Pallas kernels  53.3 us (98%)
  between operations  0.82 us (2%)
    pallas_call x1, Pallas kernels, local(): pl.pallas_call(kernel, out_shape=out_shape, in_specs=[anywhere] * 8, out_...  50.9 us
    pallas_call x1, Pallas kernels, local(): pl.pallas_call(copy_kernel, out_shape=out_shape, in_specs=[anywhere] * 5,...  2.37 us

profile of v3, /device:TPU:1, one launch (start us, length us, event | category | flops | bytes accessed | tf_op | source)
XLA Modules:
  0.0 54.1 jit_solution(16130329161177187530)
XLA Ops:
  0.6 50.9 %section.1 = (bf16[384,128]{1,0:T(8,128)(2,1)}, bf16[384,128]{1,0:T(8,128)(2,1)}, bf16[1024,256]{1,0:T(8,128)(2,1)}, bf16[2048,128]{1,0:T(8,128)(2,1)}, bf16[256,1024]{1,0:T(8,128)(2,1)}) custom-call(bf16[384,128]{1,0:T(8,128)(2,1)} %bitcast.33, bf16[384,128]{1,0:T(8,128)(2,1)} %bitcast.34, bf16[384,128]{1,0:T(8,128)(2,1)} %bitcast.35, ...), custom_call_target="tpu_custom_call" | custom-call | flops 4000000000 | bytes 8000000 | tf_op jit(solution)/shard_map/section/pallas_call | solution.py:661
  51.5 2.4 %results.1 = (bf16[384,128]{1,0:T(8,128)(2,1)}, bf16[384,128]{1,0:T(8,128)(2,1)}, bf16[1024,256]{1,0:T(8,128)(2,1)}, bf16[2048,128]{1,0:T(8,128)(2,1)}, bf16[256,1024]{1,0:T(8,128)(2,1)}) custom-call(bf16[384,128]{1,0:T(8,128)(2,1)} %get-tuple-element.15.refs_0_, bf16[384,128]{1,0:T(8,128)(2,1)} %get-tuple-element.16.refs_1_, ...), custom_call_target="tpu_custom_call" | custom-call | bytes 4000000 | tf_op jit(solution)/shard_map/results/pallas_call | solution.py:714

commit v4 on v3

--- a/solution.py
+++ b/solution.py
@@ -266,7 +266,7 @@
         return pl.ds(pl.multiple_of(i * ROWS_PAD, ROWS_PAD), ROWS_PAD)
 
     def for_slabs(slabs, step):
-        lax.fori_loop(0, slabs, lambda i, carry: step(i) or carry, 0, unroll=2)
+        lax.fori_loop(0, slabs, lambda i, carry: step(i) or carry, 0, unroll=4)
 
     def received(arr, i):
         return unpack(buf[arr, i // SLABS, i % SLABS].astype(F32))
@@ -529,10 +529,13 @@
                 near(ACTS)
                 slots_of(GRAD, ag_wait)
 
-            run_back(0, rows, pos_back, allowed_back, middle, lambda: rest(ACTS))
+            def late():
+                rest(ACTS)
+                relay()
+
+            run_back(0, rows, pos_back, allowed_back, middle, late)
             slots_rs(BACK, rs_send)
             slots_rs(BACK, rs_cross)
-            relay()
             prepare(ACTS, 2, pos_fwd)
             slots_rs(BACK, finish_back)
             near(SAVED_2, GRAD_2)
@@ -580,9 +583,12 @@
         run_back(1, rows, pos_two, allowed_two, lambda: slots_of(GRAD_2, ag_wait), nothing)
         if at_last:
             slots_rs(FORWARD, finish_forward)
+        weights(rows)
         if at_first:
             slots_rs(BACK, finish_back)
-        weights(rows)
+
+        q, k = iota((lines, lines), 1), iota((lines, lines), 0)
+        gather = jnp.where(line_of(q, width) == k, 1.0, 0.0).astype(BF16)
 
         for f, none, two in ((FORWARD, at_first, at_last), (BACK, at_last, at_first)):
             for slot in ([] if none else [0]) + ([1] if two else []):
@@ -592,8 +598,6 @@
                     tiles[at : at + ROWS_PAD, f * HEAD : (f + 1) * HEAD] = hrecv[
                         f, slot, :, ct * HEAD : (ct + 1) * HEAD
                     ]
-        q, k = iota((lines, lines), 1), iota((lines, lines), 0)
-        gather = jnp.where(line_of(q, width) == k, 1.0, 0.0).astype(BF16)
         found = nn(gather, tiles[...]).astype(BF16)
         handed[...] = found[:, FORWARD * HEAD : (FORWARD + 1) * HEAD]
         back[...] = found[:, BACK * HEAD : (BACK + 1) * HEAD]

time: 54.2 us -> 54.1 us (level)
  Pallas kernels: 53.3 us -> 52.7 us
    pallas_call x1, Pallas kernels: 50.9 us -> 50.3 us  [local(): pl.pallas_call(kernel, out_shape=out_shape, in_specs=[anywhere] * 8, out_...]
where the time goes in v4:
time: 54.1 us; the launch traced here: 53.5 us
  Pallas kernels  52.7 us (97%)
  between operations  0.82 us (2%)
    pallas_call x1, Pallas kernels, local(): pl.pallas_call(kernel, out_shape=out_shape, in_specs=[anywhere] * 8, out_...  50.3 us
    pallas_call x1, Pallas kernels, local(): pl.pallas_call(copy_kernel, out_shape=out_shape, in_specs=[anywhere] * 5,...  2.37 us

profile of v4, /device:TPU:1, one launch (start us, length us, event | category | flops | bytes accessed | tf_op | source)
XLA Modules:
  0.0 53.5 jit_solution(7449205646194537009)
XLA Ops:
  0.6 50.3 %section.1 = (bf16[384,128]{1,0:T(8,128)(2,1)}, bf16[384,128]{1,0:T(8,128)(2,1)}, bf16[1024,256]{1,0:T(8,128)(2,1)}, bf16[2048,128]{1,0:T(8,128)(2,1)}, bf16[256,1024]{1,0:T(8,128)(2,1)}) custom-call(bf16[384,128]{1,0:T(8,128)(2,1)} %bitcast.33, bf16[384,128]{1,0:T(8,128)(2,1)} %bitcast.34, bf16[384,128]{1,0:T(8,128)(2,1)} %bitcast.35, ...), custom_call_target="tpu_custom_call" | custom-call | flops 4000000000 | bytes 8000000 | tf_op jit(solution)/shard_map/section/pallas_call | solution.py:665
  51.0 2.4 %results.1 = (bf16[384,128]{1,0:T(8,128)(2,1)}, bf16[384,128]{1,0:T(8,128)(2,1)}, bf16[1024,256]{1,0:T(8,128)(2,1)}, bf16[2048,128]{1,0:T(8,128)(2,1)}, bf16[256,1024]{1,0:T(8,128)(2,1)}) custom-call(bf16[384,128]{1,0:T(8,128)(2,1)} %get-tuple-element.15.refs_0_, bf16[384,128]{1,0:T(8,128)(2,1)} %get-tuple-element.16.refs_1_, ...), custom_call_target="tpu_custom_call" | custom-call | bytes 4000000 | tf_op jit(solution)/shard_map/results/pallas_call | solution.py:718
